TPU v7x, 128 devices: a whole 4x4x4 slice. The times are simulated.
128 devices in a mesh: ox: 16 (over y, x), oy: 8 (over z, core).
Axes of the slice: x: 4, y: 4, z: 4, core: 2. Of those that a mesh axis runs over, the one named last changes fastest.
Arguments:
- atm_flux: float32 [4096, 6, 128], P(('ox', 'oy')), may hold values from -6 to 6
- pair_weight: float32 [12288, 128, 256], P(('ox', 'oy')), may hold values from -0.5 to 0.5
- pair_src: int32 [12288], P(('ox', 'oy')), may hold values from 0 to 31
- pair_dest: int32 [12288, 1], P(('ox', 'oy')), may hold values from 0 to 127; in each aligned block of 96 rows (0 to 95, 96 to 191, ...) at most 2 rows name the same one
- pair_block: int32 [12288], P(('ox', 'oy')), may hold values from 0 to 15
- ocean_state: float32 [80, 6, 256, 2048], P(None, None, 'ox', 'oy'), may hold values from -6 to 6
- land_mask: int32 [256, 2048], P('ox', 'oy'), may hold values 0 or 1
- kpp_depth: int32 [256, 2048], P('ox', 'oy'), may hold values from 1 to 79
- mixing_scale: float32 [256, 2048], P('ox', 'oy'), may hold values from 0.2 to 5
Outputs:
- ocean_out: float32 [80, 6, 256, 2048], P(None, None, 'ox', 'oy')
- atm_surface: float32 [4096, 6, 128], P(('ox', 'oy'))
Inputs may be any that keep to these rules, and one draw needn't show every extreme that they name: `pair_dest`: among the pairs of one device no ocean device is named more than 2 times, and in every draw some device names one ocean device exactly 2 times.
All inputs are finite; a program needn't handle non-finite values. No bound on the sum of `land_mask` on one device may be relied on, other than what follows from the above.
Results may differ from a plain program's by a relative error of at most 0.000094.
Values sent between devices are 32-bit elements; how exact they have to be, the bound alone decides.
A program may use at most 192 MiB of HBM per device.

v0:
```python
import jax
import jax.numpy as jnp
from jax import lax
from jax.sharding import PartitionSpec as P

HIGHEST = lax.Precision.HIGHEST
VISCOSITY = 0.025
FORCING = 0.5
BACKGROUND = 0.05


def padded_2(block, sides, width):
    for axis, dim in sides:
        count = lax.axis_size(axis)
        forward = [(i, i + 1) for i in range(count - 1)]
        backward = [(target, source) for source, target in forward]
        low = lax.ppermute(
            lax.slice_in_dim(block, block.shape[dim] - width, None, axis=dim), axis, forward
        )
        high = lax.ppermute(lax.slice_in_dim(block, 0, width, axis=dim), axis, backward)
        block = jnp.concatenate([low, block, high], axis=dim)
    return block


def laplace(padded):
    return (
        padded[..., 2:, 1:-1]
        + padded[..., :-2, 1:-1]
        + padded[..., 1:-1, 2:]
        + padded[..., 1:-1, :-2]
        - 4.0 * padded[..., 1:-1, 1:-1]
    )


def couplings(kpp_depth, mixing_scale, level_count):
    level_index = jnp.arange(level_count - 1, dtype=jnp.int32)[:, None, None]
    level_float = level_index.astype(jnp.float32)
    depth_float = kpp_depth.astype(jnp.float32)[None]
    sigma = (level_float + 1.0) / depth_float
    profile = BACKGROUND + 6.75 * sigma * (1.0 - sigma) * (1.0 - sigma)
    inside = level_index < kpp_depth[None]
    return mixing_scale[None] * jnp.where(inside, profile, BACKGROUND)


def thomas(coupling, right_side):
    levels_num = right_side.shape[0]
    zero_slab = jnp.zeros_like(coupling[0])
    bands = [zero_slab] + [coupling[k] for k in range(levels_num - 1)] + [zero_slab]
    ratio_list = []
    value_list = []
    ratio_prev = zero_slab
    value_prev = jnp.zeros_like(right_side[0])
    for k in range(levels_num):
        lower_now = -bands[k]
        upper_now = -bands[k + 1]
        diagonal_now = 1.0 + bands[k] + bands[k + 1]
        denominator = diagonal_now - lower_now * ratio_prev
        ratio_now = upper_now / denominator
        value_now = (right_side[k] - lower_now[None] * value_prev) / denominator[None]
        ratio_list.append(ratio_now)
        value_list.append(value_now)
        ratio_prev = ratio_now
        value_prev = value_now
    solved_list = [None] * levels_num
    carried = jnp.zeros_like(right_side[0])
    for k in range(levels_num - 1, -1, -1):
        carried = value_list[k] - ratio_list[k][None] * carried
        solved_list[k] = carried
    return jnp.stack(solved_list, axis=0)


def with_rims(values):
    return padded_2(values, (("ox", 2), ("oy", 3)), 1)


def shards(
    atm_flux,
    pair_weight,
    pair_src,
    pair_dest,
    pair_block,
    ocean_state,
    land_mask,
    kpp_depth,
    mixing_scale,
):
    count_x = lax.axis_size("ox")
    count_y = lax.axis_size("oy")
    devices_all = count_x * count_y
    pair_count = pair_weight.shape[0]
    slot_count = max(2, 8 * pair_count // (3 * devices_all))
    total_slots = devices_all * slot_count
    atm_blocks = atm_flux.shape[0]
    fields_num = atm_flux.shape[1]
    atm_width = atm_flux.shape[2]
    levels_num = ocean_state.shape[0]
    tile_rows = ocean_state.shape[2]
    tile_cols = ocean_state.shape[3]
    wet_cells = land_mask.astype(jnp.float32)
    masked = wet_cells * ocean_state
    first_pass = wet_cells * laplace(with_rims(masked))
    second_pass = wet_cells * laplace(with_rims(first_pass))
    destination = pair_dest[:, 0]
    pair_order = jnp.arange(pair_count, dtype=jnp.int32)
    earlier_same = (destination[:, None] == destination[None, :]) & (
        pair_order[None, :] < pair_order[:, None]
    )
    slot_rank = jnp.sum(earlier_same.astype(jnp.int32), axis=1)
    slot_index = destination * slot_count + slot_rank
    slot_numbers = jnp.arange(total_slots, dtype=jnp.int32)
    placing = slot_numbers[:, None] == slot_index[None, :]
    placing_float = placing.astype(jnp.float32)
    source_pick = (pair_src[:, None] == jnp.arange(atm_blocks, dtype=jnp.int32)[None, :]).astype(
        jnp.float32
    )
    gathered = jnp.dot(
        source_pick, atm_flux.reshape(atm_blocks, fields_num * atm_width), precision=HIGHEST
    )
    gathered = gathered.reshape(pair_count, fields_num, atm_width)
    contribution = jnp.einsum("gfa,gao->gfo", gathered, pair_weight, precision=HIGHEST)
    outgoing = jnp.dot(
        placing_float, contribution.reshape(pair_count, fields_num * tile_cols), precision=HIGHEST
    )
    outgoing_ids = jnp.sum(placing.astype(jnp.int32) * (pair_block + 1)[None, :], axis=1) - 1
    arrived, arrived_ids = (
        lax.all_to_all(
            outgoing.reshape(devices_all, slot_count, fields_num * tile_cols),
            ("ox", "oy"),
            split_axis=0,
            concat_axis=0,
            tiled=True,
        ),
        lax.all_to_all(
            outgoing_ids.reshape(devices_all, slot_count),
            ("ox", "oy"),
            split_axis=0,
            concat_axis=0,
            tiled=True,
        ),
    )
    arrived = arrived.reshape(total_slots, fields_num * tile_cols)
    arrived_ids = arrived_ids.reshape(total_slots)
    row_pick = (arrived_ids[:, None] == jnp.arange(tile_rows, dtype=jnp.int32)[None, :]).astype(
        jnp.float32
    )
    flux_rows = jnp.dot(row_pick.T, arrived, precision=HIGHEST)
    surface_flux = jnp.transpose(flux_rows.reshape(tile_rows, fields_num, tile_cols), (1, 0, 2))
    right_side = masked.at[0].add(FORCING * wet_cells * surface_flux)
    mixed_state = thomas(couplings(kpp_depth, mixing_scale, levels_num), right_side)
    ocean_out = mixed_state - VISCOSITY * second_pass
    surface_rows = jnp.transpose(ocean_out[0], (1, 0, 2)).reshape(tile_rows, fields_num * tile_cols)
    reply_rows = jnp.dot(row_pick, surface_rows, precision=HIGHEST)
    answered = lax.all_to_all(
        reply_rows.reshape(devices_all, slot_count, fields_num * tile_cols),
        ("ox", "oy"),
        split_axis=0,
        concat_axis=0,
        tiled=True,
    )
    answered = answered.reshape(total_slots, fields_num * tile_cols)
    per_pair = jnp.dot(placing_float.T, answered, precision=HIGHEST).reshape(
        pair_count, fields_num, tile_cols
    )
    atm_terms = jnp.einsum("gfo,gao->gfa", per_pair, pair_weight, precision=HIGHEST)
    atm_surface = jnp.dot(
        source_pick.T, atm_terms.reshape(pair_count, fields_num * atm_width), precision=HIGHEST
    )
    return (ocean_out, atm_surface.reshape(atm_blocks, fields_num, atm_width))


def solution(mesh):
    return jax.shard_map(
        shards,
        mesh=mesh,
        in_specs=(
            P(("ox", "oy"), None, None),
            P(("ox", "oy"), None, None),
            P(("ox", "oy")),
            P(("ox", "oy"), None),
            P(("ox", "oy")),
            P(None, None, "ox", "oy"),
            P("ox", "oy"),
            P("ox", "oy"),
            P("ox", "oy"),
        ),
        out_specs=(P(None, None, "ox", "oy"), P(("ox", "oy"), None, None)),
        check_vma=False,
    )
```

profile of v0, /device:TPU:1, one launch (start us, length us, event | category | flops | bytes accessed | tf_op | source)
XLA Modules:
  0.0 363.5 jit_solution(6308803260314367134)
XLA Ops:
  0.6 0.9 convert_reduce_fusion
  2.9 0.8 sub.6275
  3.7 12.0 %all-to-all-start = ((s32[128,1,2]{2,1,0:T(1,128)}), s32[128,1,2]{2,1,0:T(1,128)}, u32[]{:S(2)}, u32[]{:S(2)}) async-start(s32[128,1,2]{2,1,0:T(1,128)} %bitcast.1), calls=%async_computation | async-start | bytes 131072 | tf_op jit(solution)/shard_map/all_to_all | solution.py:133
  15.6 0.7 convert_element_type.21
  16.4 4.5 %broadcast_multiply_fusion = f32[80,6,16,256]{3,2,1,0:T(8,128)S(1)} fusion(f32[80,6,16,256]{3,2,1,0:T(8,128)} %param.16, f32[16,256]{1,0:T(8,128)S(1)} %convert_element_type.21), kind=kLoop, calls=%fused_computation.30 | loop fusion | flops 1966080 | bytes 15745024 | tf_op jit(solution)/shard_map/mul | solution.py:100
  20.9 4.0 %copy-done.2 = f32[80,6,16,256]{3,2,1,0:T(8,128)} copy-done((f32[80,6,16,256]{3,2,1,0:T(8,128)}, f32[80,6,16,256]{3,2,1,0:T(8,128)S(1)}, u32[]{:S(2)}) %copy-start.2) | copy-done | bytes 7864344
  24.9 1.6 fusion.437
  26.5 4.1 %collective-permute-start.1 = (f32[80,6,1,256]{3,2,1,0:T(1,128)}, f32[80,6,1,256]{3,2,1,0:T(1,128)}, u32[]{:S(2)}, u32[]{:S(2)}) collective-permute-start(f32[80,6,1,256]{3,2,1,0:T(1,128)} %get-tuple-element.257), channel_id=1, source_target_pairs={{0,8},{8,16},{16,24},{24,32},{32,40},{40,48},{48,56},{56,64},{64,7... | collective-permute-start | bytes 1474568 | tf_op jit(solution)/shard_map/ppermute | solution.py:17
  30.6 1.5 collective-permute-start
  33.7 0.7 negate_bitcast_fusion.33
  34.4 0.7 negate_bitcast_fusion.35
  35.5 6.1 %fusion.19 = f32[96,6,256]{2,1,0:T(8,128)S(1)} fusion(f32[96,128,256]{2,1,0:T(8,128)S(1)} %copy-done.3, f32[96,6,128]{2,0,1:T(8,128)S(1)} %fusion.24), kind=kOutput, calls=%fused_computation.41 | convolution fusion | flops 226492416 | bytes 13467648 | tf_op jit(solution)/shard_map/gfa,gao->gfo/dot_general | solution.py:120
  50.7 0.7 negate_bitcast_fusion.31
  52.1 0.8 fusion.312
  62.9 1.5 fusion.110
  64.4 9.5 %pad_maximum_fusion = f32[80,6,18,256]{3,2,1,0:T(8,128)} fusion(f32[80,6,1,256]{3,2,1,0:T(1,128)} %collective-permute-done, f32[80,6,16,256]{3,2,1,0:T(8,128)} %copy-done.2, f32[80,6,1,256]{3,2,1,0:T(1,128)} %collective-permute-done.1), kind=kLoop, calls=%fused_computation | loop fusion | flops 4423680 | bytes 17694720 | tf_op jit(solution)/shard_map/concatenate | solution.py:21
  73.9 10.2 %fusion.435 = (f32[80,6,18,1]{3,2,1,0:T(8,128)}, f32[80,6,18,1]{3,2,1,0:T(8,128)}) fusion(f32[80,6,18,256]{3,2,1,0:T(8,128)} %pad_maximum_fusion), kind=kLoop, calls=%fused_computation.1026 | loop fusion | bytes 138240 | tf_op jit(solution)/shard_map/slice | solution.py:20
  84.2 4.3 %copy.45 = f32[80,6,18,1]{0,3,2,1:T(1,128)S(1)} copy(f32[80,6,18,1]{3,2,1,0:T(8,128)} %get-tuple-element.253) | data formatting | bytes 69120 | tf_op jit(solution)/shard_map/slice | solution.py:20
  88.4 4.3 %copy.47 = f32[80,6,18,1]{0,3,2,1:T(1,128)S(1)} copy(f32[80,6,18,1]{3,2,1,0:T(8,128)} %get-tuple-element.254) | data formatting | bytes 69120 | tf_op jit(solution)/shard_map/slice | solution.py:18
  92.7 3.7 %collective-permute-start.3 = (f32[80,6,18,1]{0,3,2,1:T(1,128)S(1)}, f32[80,6,18,1]{0,3,2,1:T(1,128)S(1)}, u32[]{:S(2)}, u32[]{:S(2)}) collective-permute-start(f32[80,6,18,1]{0,3,2,1:T(1,128)S(1)} %copy.47), channel_id=1, source_target_pairs={{0,1},{1,2},{2,3},{3,4},{4,5},{5,6},{6,7},{8,9},{9,10},{10,11},{11... | collective-permute-start | bytes 103688 | tf_op jit(solution)/shard_map/ppermute | solution.py:17
  96.5 1.9 collective-permute-start.2
  99.0 2.9 collective-permute-done.2
  101.9 4.2 %copy.46 = f32[80,6,18,1]{3,2,1,0:T(8,128)} copy(f32[80,6,18,1]{0,3,2,1:T(1,128)S(1)} %collective-permute-done.2) | data formatting | bytes 69120 | tf_op jit(solution)/shard_map/ppermute | solution.py:20
  106.1 4.1 %copy.48 = f32[80,6,18,1]{3,2,1,0:T(8,128)} copy(f32[80,6,18,1]{0,3,2,1:T(1,128)S(1)} %collective-permute-done.3) | data formatting | bytes 69120 | tf_op jit(solution)/shard_map/ppermute | solution.py:17
  110.2 23.2 %fusion.9 = f32[80,6,16,256]{3,2,1,0:T(8,128)} fusion(f32[80,6,18,1]{3,2,1,0:T(8,128)} %copy.48, f32[80,6,1,256]{3,2,1,0:T(1,128)} %collective-permute-done, f32[80,6,16,256]{3,2,1,0:T(8,128)} %copy-done.2, f32[80,6,1,256]{3,2,1,0:T(1,128)} %collective-permute-done.1, f32[80,6,18,1]{3,2,1,0:T(8,128)} %copy.46, f32[16,256]{1,0:T(8,128)S(1)} %copy-done.20), kind=kLoop, calls=%fused_computation.20 | loop fusion | flops 27525120 | bytes 16797184 | tf_op jit(solution)/shard_map/mul | solution.py:101
  133.4 5.2 %fusion.436 = (f32[80,6,1,256]{3,2,1,0:T(1,128)}, f32[80,6,1,256]{3,2,1,0:T(1,128)}) fusion(f32[80,6,16,256]{3,2,1,0:T(8,128)} %fusion.9), kind=kLoop, calls=%fused_computation.1027 | loop fusion | bytes 1966080 | tf_op jit(solution)/shard_map/slice | solution.py:18
  138.6 4.3 %collective-permute-start.5 = (f32[80,6,1,256]{3,2,1,0:T(1,128)}, f32[80,6,1,256]{3,2,1,0:T(1,128)S(1)}, u32[]{:S(2)}, u32[]{:S(2)}) collective-permute-start(f32[80,6,1,256]{3,2,1,0:T(1,128)} %get-tuple-element.255), channel_id=1, source_target_pairs={{0,8},{8,16},{16,24},{24,32},{32,40},{40,48},{48,56},{56,64},{64,7... | collective-permute-start | bytes 1474568 | tf_op jit(solution)/shard_map/ppermute | solution.py:17
  142.9 1.3 collective-permute-start.4
  144.9 2.4 copy.43
  147.2 11.3 %all-to-all-start.1 = ((f32[128,2,1536]{2,1,0:T(2,128)}), f32[128,2,1536]{2,1,0:T(2,128)S(1)}, u32[]{:S(2)}, u32[]{:S(2)}) async-start(f32[128,2,1536]{2,1,0:T(2,128)} %copy.43), calls=%async_computation.1 | async-start | bytes 3145728 | tf_op jit(solution)/shard_map/all_to_all | solution.py:126
  158.5 1.6 divide_multiply_fusion.43
  160.2 9.0 %pad_maximum_fusion.1 = f32[80,6,18,256]{3,2,1,0:T(8,128)} fusion(f32[80,6,1,256]{3,2,1,0:T(1,128)} %collective-permute-done.4, f32[80,6,16,256]{3,2,1,0:T(8,128)} %fusion.9, f32[80,6,1,256]{3,2,1,0:T(1,128)S(1)} %collective-permute-done.5), kind=kLoop, calls=%fused_computation.1 | loop fusion | flops 4423680 | bytes 17694720 | tf_op jit(solution)/shard_map/concatenate | solution.py:21
  169.2 10.4 %fusion.434 = (f32[80,6,18,1]{3,2,1,0:T(8,128)}, f32[80,6,18,1]{3,2,1,0:T(8,128)}) fusion(f32[80,6,18,256]{3,2,1,0:T(8,128)} %pad_maximum_fusion.1), kind=kLoop, calls=%fused_computation.1025 | loop fusion | bytes 138240 | tf_op jit(solution)/shard_map/slice | solution.py:20
  179.6 4.3 %copy.49 = f32[80,6,18,1]{0,3,2,1:T(1,128)S(1)} copy(f32[80,6,18,1]{3,2,1,0:T(8,128)} %get-tuple-element.251) | data formatting | bytes 69120 | tf_op jit(solution)/shard_map/slice | solution.py:20
  183.8 4.3 %copy.51 = f32[80,6,18,1]{0,3,2,1:T(1,128)S(1)} copy(f32[80,6,18,1]{3,2,1,0:T(8,128)} %get-tuple-element.252) | data formatting | bytes 69120 | tf_op jit(solution)/shard_map/slice | solution.py:18
  188.1 3.7 %collective-permute-start.7 = (f32[80,6,18,1]{0,3,2,1:T(1,128)S(1)}, f32[80,6,18,1]{0,3,2,1:T(1,128)S(1)}, u32[]{:S(2)}, u32[]{:S(2)}) collective-permute-start(f32[80,6,18,1]{0,3,2,1:T(1,128)S(1)} %copy.51), channel_id=1, source_target_pairs={{0,1},{1,2},{2,3},{3,4},{4,5},{5,6},{6,7},{8,9},{9,10},{10,11},{11... | collective-permute-start | bytes 103688 | tf_op jit(solution)/shard_map/ppermute | solution.py:17
  191.8 1.9 collective-permute-start.6
  194.3 1.4 copy.53
  196.3 1.6 reduce.5
  197.9 0.7 eq.101
  198.6 4.2 %copy.50 = f32[80,6,18,1]{3,2,1,0:T(8,128)} copy(f32[80,6,18,1]{0,3,2,1:T(1,128)S(1)} %collective-permute-done.6) | data formatting | bytes 69120 | tf_op jit(solution)/shard_map/ppermute | solution.py:20
  202.8 4.2 %copy.52 = f32[80,6,18,1]{3,2,1,0:T(8,128)} copy(f32[80,6,18,1]{0,3,2,1:T(1,128)S(1)} %collective-permute-done.7) | data formatting | bytes 69120 | tf_op jit(solution)/shard_map/ppermute | solution.py:17
  207.0 2.2 reshape.231
  209.2 1.9 copy.44
  211.4 4.0 %fusion.65 = (f32[6,16,256]{2,1,0:T(8,128)S(1)}, f32[6,16,256]{2,1,0:T(8,128)S(1)}, f32[6,16,256]{2,1,0:T(8,128)S(1)}, f32[6,16,256]{2,1,0:T(8,128)S(1)}, f32[6,...) fusion(f32[80,6,16,256]{3,2,1,0:T(8,128)} %copy-done.2, ...), kind=kOutput, calls=%fused_computation.208 | convolution fusion | flops 78671872 | bytes 8782848 | tf_op jit(solution)/shard_map/dot_general | solution.py:146
  215.9 6.3 %constant_dynamic-update-slice_fusion.79 = (f32[80,6,16,256]{3,2,1,0:T(8,128)}, f32[6,16,256]{2,1,0:T(8,128)S(1)}, f32[6,16,256]{2,1,0:T(8,128)S(1)}, f32[6,16,2...) fusion(f32[16,256]{1,0:T(8,128)} %get-tuple-element.308, ...), kind=kLoop, calls=%fused_computation.126 | loop fusion | flops 8650751 | bytes 15712256
  222.2 1.4 constant_dynamic-update-slice_fusion.78
  224.2 1.4 constant_dynamic-update-slice_fusion.76
  226.2 1.4 constant_dynamic-update-slice_fusion.74
  228.2 1.4 constant_dynamic-update-slice_fusion.72
  230.2 1.4 constant_dynamic-update-slice_fusion.70
  232.3 1.4 constant_dynamic-update-slice_fusion.68
  234.3 1.4 constant_dynamic-update-slice_fusion.66
  236.3 1.4 constant_dynamic-update-slice_fusion.64
  238.3 5.5 %constant_dynamic-update-slice_fusion.62 = (f32[80,6,16,256]{3,2,1,0:T(8,128)}, f32[1,6,16,256]{3,2,1,0:T(8,128)S(1)}, f32[1,6,16,256]{3,2,1,0:T(8,128)S(1)}, f3...) fusion(f32[80,6,16,256]{3,2,1,0:T(8,128)} %constant_dynamic-upd, ...), kind=kLoop, calls=%fused_computation.109 | loop fusion | flops 8921088 | bytes 14057472
  283.9 25.4 %fusion.4 = f32[80,6,16,256]{3,2,1,0:T(8,128)} fusion(f32[80,6,16,256]{3,2,1,0:T(8,128)} %constant_dynamic-update-slice_fusion, f32[80,6,18,1]{3,2,1,0:T(8,128)} %copy.52, f32[80,6,1,256]{3,2,1,0:T(1,128)} %collective-permute-done.4, f32[80,6,16,256]{3,2,1,0:T(8,128)} %fusion.9, f32[80,6,1,256]{3,2,1,0:T(1,128)S(1)} %collective-permute-done.5, ...), kind=kLoop, calls=%fused_computation.7 | loop fusion | flops 31457280 | bytes 24661504 | tf_op jit(solution)/shard_map/sub | solution.py:150
  309.3 0.9 slice_bitcast_fusion
  310.3 0.8 fusion.242
  311.2 1.2 copy.55
  312.4 34.3 %all_to_all.16 = f32[128,2,1536]{2,1,0:T(2,128)S(1)} all-to-all(f32[128,2,1536]{2,1,0:T(2,128)S(1)} %copy.55), channel_id=1, replica_groups=mesh['ox'=16,'oy'=8] {'ox','oy'}, dimensions={0} | all-to-all | bytes 3145728 | tf_op jit(solution)/shard_map/all_to_all | solution.py:153
  346.7 1.1 reshape.234
  348.3 1.0 fusion.108
  349.3 13.1 %fusion.17 = f32[96,6,128]{2,1,0:T(8,128)S(1)} fusion(f32[96,128,256]{2,1,0:T(8,128)} %param.12, f32[96,6,256]{2,0,1:T(8,128)S(1)} %fusion.108), kind=kOutput, calls=%fused_computation.39 | convolution fusion | flops 226492416 | bytes 13467648 | tf_op jit(solution)/shard_map/gfo,gao->gfa/dot_general | solution.py:164
  362.3 0.9 fusion.21
  (318 shorter events, 71.2 us)
Async XLA Ops:
  0.6 34.6 %copy-start = (f32[32,6,128]{2,0,1:T(8,128)S(1)}, f32[32,6,128]{2,0,1:T(8,128)}, u32[]{:S(2)}) copy-start(f32[32,6,128]{2,0,1:T(8,128)} %param.11) | copy-start | bytes 294916
  3.7 143.6 %all-to-all-start = ((s32[128,1,2]{2,1,0:T(1,128)}), s32[128,1,2]{2,1,0:T(1,128)}, u32[]{:S(2)}, u32[]{:S(2)}) async-start(s32[128,1,2]{2,1,0:T(1,128)} %bitcast.1), calls=%async_computation | async-start | bytes 131072 | tf_op jit(solution)/shard_map/all_to_all | solution.py:133
  16.3 4.6 %copy-start.19 = (f32[16,256]{1,0:T(8,128)}, f32[16,256]{1,0:T(8,128)S(1)}, u32[]{:S(2)}) copy-start(f32[16,256]{1,0:T(8,128)S(1)} %convert_element_type.21) | copy-start | bytes 49156
  16.3 16.3 %copy-start.86 = (s32[16,256]{1,0:T(8,128)S(1)}, s32[16,256]{1,0:T(8,128)}, u32[]{:S(2)}) copy-start(s32[16,256]{1,0:T(8,128)} %param.18) | copy-start | bytes 49156
  16.3 16.3 %copy-start.88 = (f32[16,256]{1,0:T(8,128)S(1)}, f32[16,256]{1,0:T(8,128)}, u32[]{:S(2)}) copy-start(f32[16,256]{1,0:T(8,128)} %param.19) | copy-start | bytes 49156
  16.3 18.8 %copy-start.92 = (s32[96]{0:T(128)S(1)}, s32[96]{0:T(128)}, u32[]{:S(2)}) copy-start(s32[96]{0:T(128)} %param.13) | copy-start | bytes 1156
  16.4 19.2 %copy-start.3 = (f32[96,128,256]{2,1,0:T(8,128)S(1)}, f32[96,128,256]{2,1,0:T(8,128)}, u32[]{:S(2)}) copy-start(f32[96,128,256]{2,1,0:T(8,128)} %param.12) | copy-start | bytes 37748740
  26.5 37.9 %collective-permute-start.1 = (f32[80,6,1,256]{3,2,1,0:T(1,128)}, f32[80,6,1,256]{3,2,1,0:T(1,128)}, u32[]{:S(2)}, u32[]{:S(2)}) collective-permute-start(f32[80,6,1,256]{3,2,1,0:T(1,128)} %get-tuple-element.257), channel_id=1, source_target_pairs={{0,8},{8,16},{16,24},{24,32},{32,40},{40,48},{48,56},{56,64},{64,7... | collective-permute-start | bytes 1474568 | tf_op jit(solution)/shard_map/ppermute | solution.py:17
  30.6 33.8 %collective-permute-start = (f32[80,6,1,256]{3,2,1,0:T(1,128)}, f32[80,6,1,256]{3,2,1,0:T(1,128)}, u32[]{:S(2)}, u32[]{:S(2)}) collective-permute-start(f32[80,6,1,256]{3,2,1,0:T(1,128)} %get-tuple-element.258), channel_id=1, source_target_pairs={{8,0},{16,8},{24,16},{32,24},{40,32},{48,40},{56,48},{64,56},{72,6... | collective-permute-start | bytes 1474568 | tf_op jit(solution)/shard_map/ppermute | solution.py:20
  33.7 8.2 %copy-start.84 = (f32[1,16,256]{2,1,0:T(8,128)}, f32[1,16,256]{2,1,0:T(8,128)S(1)}, u32[]{:S(2)}) copy-start(f32[1,16,256]{2,1,0:T(8,128)S(1)} %get-tuple-element.86) | copy-start | bytes 49156
  42.5 168.6 %copy-start.34 = (f32[1,16,256]{2,1,0:T(8,128)}, f32[1,16,256]{2,1,0:T(8,128)S(1)}, u32[]{:S(2)}) copy-start(f32[1,16,256]{2,1,0:T(8,128)S(1)} %get-tuple-element.89) | copy-start | bytes 49156
  43.1 168.0 %copy-start.36 = (f32[1,16,256]{2,1,0:T(8,128)}, f32[1,16,256]{2,1,0:T(8,128)S(1)}, u32[]{:S(2)}) copy-start(f32[1,16,256]{2,1,0:T(8,128)S(1)} %get-tuple-element.92) | copy-start | bytes 49156
  43.8 167.3 %copy-start.38 = (f32[1,16,256]{2,1,0:T(8,128)}, f32[1,16,256]{2,1,0:T(8,128)S(1)}, u32[]{:S(2)}) copy-start(f32[1,16,256]{2,1,0:T(8,128)S(1)} %get-tuple-element.95) | copy-start | bytes 49156
  44.4 166.7 %copy-start.40 = (f32[1,16,256]{2,1,0:T(8,128)}, f32[1,16,256]{2,1,0:T(8,128)S(1)}, u32[]{:S(2)}) copy-start(f32[1,16,256]{2,1,0:T(8,128)S(1)} %get-tuple-element.98) | copy-start | bytes 49156
  45.0 166.1 %copy-start.42 = (f32[1,16,256]{2,1,0:T(8,128)}, f32[1,16,256]{2,1,0:T(8,128)S(1)}, u32[]{:S(2)}) copy-start(f32[1,16,256]{2,1,0:T(8,128)S(1)} %get-tuple-element.101) | copy-start | bytes 49156
  45.7 28.3 %copy-start.44 = (f32[1,16,256]{2,1,0:T(8,128)}, f32[1,16,256]{2,1,0:T(8,128)S(1)}, u32[]{:S(2)}) copy-start(f32[1,16,256]{2,1,0:T(8,128)S(1)} %get-tuple-element.104) | copy-start | bytes 49156
  46.3 15.4 %copy-start.47 = (f32[1,16,256]{2,1,0:T(8,128)}, f32[1,16,256]{2,1,0:T(8,128)S(1)}, u32[]{:S(2)}) copy-start(f32[1,16,256]{2,1,0:T(8,128)S(1)} %get-tuple-element.107) | copy-start | bytes 49156
  46.9 14.7 %copy-start.49 = (f32[1,16,256]{2,1,0:T(8,128)}, f32[1,16,256]{2,1,0:T(8,128)S(1)}, u32[]{:S(2)}) copy-start(f32[1,16,256]{2,1,0:T(8,128)S(1)} %get-tuple-element.109) | copy-start | bytes 49156
  47.5 14.1 %copy-start.51 = (f32[1,16,256]{2,1,0:T(8,128)}, f32[1,16,256]{2,1,0:T(8,128)S(1)}, u32[]{:S(2)}) copy-start(f32[1,16,256]{2,1,0:T(8,128)S(1)} %get-tuple-element.111) | copy-start | bytes 49156
  48.8 12.9 %copy-start.53 = (f32[1,16,256]{2,1,0:T(8,128)}, f32[1,16,256]{2,1,0:T(8,128)S(1)}, u32[]{:S(2)}) copy-start(f32[1,16,256]{2,1,0:T(8,128)S(1)} %get-tuple-element.115) | copy-start | bytes 49156
  49.4 12.3 %copy-start.55 = (f32[1,16,256]{2,1,0:T(8,128)}, f32[1,16,256]{2,1,0:T(8,128)S(1)}, u32[]{:S(2)}) copy-start(f32[1,16,256]{2,1,0:T(8,128)S(1)} %get-tuple-element.117) | copy-start | bytes 49156
  50.0 11.7 %copy-start.56 = (f32[1,16,256]{2,1,0:T(8,128)}, f32[1,16,256]{2,1,0:T(8,128)S(1)}, u32[]{:S(2)}) copy-start(f32[1,16,256]{2,1,0:T(8,128)S(1)} %get-tuple-element.119) | copy-start | bytes 49156
  51.4 10.3 %copy-start.57 = (f32[1,16,256]{2,1,0:T(8,128)}, f32[1,16,256]{2,1,0:T(8,128)S(1)}, u32[]{:S(2)}) copy-start(f32[1,16,256]{2,1,0:T(8,128)S(1)} %get-tuple-element.307) | copy-start | bytes 49156
  52.1 9.6 %copy-start.58 = (f32[1,16,256]{2,1,0:T(8,128)}, f32[1,16,256]{2,1,0:T(8,128)S(1)}, u32[]{:S(2)}) copy-start(f32[1,16,256]{2,1,0:T(8,128)S(1)} %get-tuple-element.125) | copy-start | bytes 49156
  54.2 7.5 %copy-start.59 = (f32[1,16,256]{2,1,0:T(8,128)}, f32[1,16,256]{2,1,0:T(8,128)S(1)}, u32[]{:S(2)}) copy-start(f32[1,16,256]{2,1,0:T(8,128)S(1)} %get-tuple-element.131) | copy-start | bytes 49156
  54.8 6.9 %copy-start.60 = (f32[1,16,256]{2,1,0:T(8,128)}, f32[1,16,256]{2,1,0:T(8,128)S(1)}, u32[]{:S(2)}) copy-start(f32[1,16,256]{2,1,0:T(8,128)S(1)} %get-tuple-element.133) | copy-start | bytes 49156
  55.5 6.3 %copy-start.61 = (f32[1,16,256]{2,1,0:T(8,128)}, f32[1,16,256]{2,1,0:T(8,128)S(1)}, u32[]{:S(2)}) copy-start(f32[1,16,256]{2,1,0:T(8,128)S(1)} %get-tuple-element.135) | copy-start | bytes 49156
  56.7 5.1 %copy-start.62 = (f32[1,16,256]{2,1,0:T(8,128)}, f32[1,16,256]{2,1,0:T(8,128)S(1)}, u32[]{:S(2)}) copy-start(f32[1,16,256]{2,1,0:T(8,128)S(1)} %get-tuple-element.139) | copy-start | bytes 49156
  57.3 4.4 %copy-start.63 = (f32[1,16,256]{2,1,0:T(8,128)}, f32[1,16,256]{2,1,0:T(8,128)S(1)}, u32[]{:S(2)}) copy-start(f32[1,16,256]{2,1,0:T(8,128)S(1)} %get-tuple-element.141) | copy-start | bytes 49156
  84.2 14.2 %copy-start.69 = (f32[1,16,256]{2,1,0:T(8,128)S(1)}, f32[1,16,256]{2,1,0:T(8,128)}, u32[]{:S(2)}) copy-start(f32[1,16,256]{2,1,0:T(8,128)} %get-tuple-element.157) | copy-start | bytes 49156
  88.4 21.8 %copy-start.20 = (f32[16,256]{1,0:T(8,128)S(1)}, f32[16,256]{1,0:T(8,128)}, u32[]{:S(2)}) copy-start(f32[16,256]{1,0:T(8,128)} %copy-done.19) | copy-start | bytes 49156
  92.7 13.4 %collective-permute-start.3 = (f32[80,6,18,1]{0,3,2,1:T(1,128)S(1)}, f32[80,6,18,1]{0,3,2,1:T(1,128)S(1)}, u32[]{:S(2)}, u32[]{:S(2)}) collective-permute-start(f32[80,6,18,1]{0,3,2,1:T(1,128)S(1)} %copy.47), channel_id=1, source_target_pairs={{0,1},{1,2},{2,3},{3,4},{4,5},{5,6},{6,7},{8,9},{9,10},{10,11},{11... | collective-permute-start | bytes 103688 | tf_op jit(solution)/shard_map/ppermute | solution.py:17
  96.5 5.5 %collective-permute-start.2 = (f32[80,6,18,1]{0,3,2,1:T(1,128)S(1)}, f32[80,6,18,1]{0,3,2,1:T(1,128)S(1)}, u32[]{:S(2)}, u32[]{:S(2)}) collective-permute-start(f32[80,6,18,1]{0,3,2,1:T(1,128)S(1)} %copy.45), channel_id=1, source_target_pairs={{1,0},{2,1},{3,2},{4,3},{5,4},{6,5},{7,6},{9,8},{10,9},{11,10},{12... | collective-permute-start | bytes 103688 | tf_op jit(solution)/shard_map/ppermute | solution.py:20
  99.0 45.2 %copy-start.70 = (f32[1,16,256]{2,1,0:T(8,128)}, f32[1,16,256]{2,1,0:T(8,128)S(1)}, u32[]{:S(2)}) copy-start(f32[1,16,256]{2,1,0:T(8,128)S(1)} %get-tuple-element.159) | copy-start | bytes 49156
  138.6 21.5 %collective-permute-start.5 = (f32[80,6,1,256]{3,2,1,0:T(1,128)}, f32[80,6,1,256]{3,2,1,0:T(1,128)S(1)}, u32[]{:S(2)}, u32[]{:S(2)}) collective-permute-start(f32[80,6,1,256]{3,2,1,0:T(1,128)} %get-tuple-element.255), channel_id=1, source_target_pairs={{0,8},{8,16},{16,24},{24,32},{32,40},{40,48},{48,56},{56,64},{64,7... | collective-permute-start | bytes 1474568 | tf_op jit(solution)/shard_map/ppermute | solution.py:17
  142.9 17.3 %collective-permute-start.4 = (f32[80,6,1,256]{3,2,1,0:T(1,128)}, f32[80,6,1,256]{3,2,1,0:T(1,128)}, u32[]{:S(2)}, u32[]{:S(2)}) collective-permute-start(f32[80,6,1,256]{3,2,1,0:T(1,128)} %get-tuple-element.256), channel_id=1, source_target_pairs={{8,0},{16,8},{24,16},{32,24},{40,32},{48,40},{56,48},{64,56},{72,6... | collective-permute-start | bytes 1474568 | tf_op jit(solution)/shard_map/ppermute | solution.py:20
  147.2 59.7 %all-to-all-start.1 = ((f32[128,2,1536]{2,1,0:T(2,128)}), f32[128,2,1536]{2,1,0:T(2,128)S(1)}, u32[]{:S(2)}, u32[]{:S(2)}) async-start(f32[128,2,1536]{2,1,0:T(2,128)} %copy.43), calls=%async_computation.1 | async-start | bytes 3145728 | tf_op jit(solution)/shard_map/all_to_all | solution.py:126
  179.6 14.1 %copy-start.87 = (s32[16,256]{1,0:T(8,128)S(1)}, s32[16,256]{1,0:T(8,128)}, u32[]{:S(2)}) copy-start(s32[16,256]{1,0:T(8,128)} %param.17) | copy-start | bytes 49156
  188.1 14.7 %collective-permute-start.7 = (f32[80,6,18,1]{0,3,2,1:T(1,128)S(1)}, f32[80,6,18,1]{0,3,2,1:T(1,128)S(1)}, u32[]{:S(2)}, u32[]{:S(2)}) collective-permute-start(f32[80,6,18,1]{0,3,2,1:T(1,128)S(1)} %copy.51), channel_id=1, source_target_pairs={{0,1},{1,2},{2,3},{3,4},{4,5},{5,6},{6,7},{8,9},{9,10},{10,11},{11... | collective-permute-start | bytes 103688 | tf_op jit(solution)/shard_map/ppermute | solution.py:17
  191.8 6.9 %collective-permute-start.6 = (f32[80,6,18,1]{0,3,2,1:T(1,128)S(1)}, f32[80,6,18,1]{0,3,2,1:T(1,128)S(1)}, u32[]{:S(2)}, u32[]{:S(2)}) collective-permute-start(f32[80,6,18,1]{0,3,2,1:T(1,128)S(1)} %copy.49), channel_id=1, source_target_pairs={{1,0},{2,1},{3,2},{4,3},{5,4},{6,5},{7,6},{9,8},{10,9},{11,10},{12... | collective-permute-start | bytes 103688 | tf_op jit(solution)/shard_map/ppermute | solution.py:20
  198.6 12.5 %copy-start.45 = (f32[1,16,256]{2,1,0:T(8,128)S(1)}, f32[1,16,256]{2,1,0:T(8,128)}, u32[]{:S(2)}) copy-start(f32[1,16,256]{2,1,0:T(8,128)} %copy-done.44) | copy-start | bytes 49156
  211.1 4.3 %copy-start.4 = (f32[16,256]{1,0:T(8,128)S(1)}, f32[16,256]{1,0:T(8,128)}, u32[]{:S(2)}) copy-start(f32[16,256]{1,0:T(8,128)} %get-tuple-element.303) | copy-start | bytes 49156
  211.1 4.3 %copy-start.5 = (f32[16,256]{1,0:T(8,128)S(1)}, f32[16,256]{1,0:T(8,128)}, u32[]{:S(2)}) copy-start(f32[16,256]{1,0:T(8,128)} %get-tuple-element.180) | copy-start | bytes 49156
  211.1 4.3 %copy-start.6 = (f32[16,256]{1,0:T(8,128)S(1)}, f32[16,256]{1,0:T(8,128)}, u32[]{:S(2)}) copy-start(f32[16,256]{1,0:T(8,128)} %get-tuple-element.184) | copy-start | bytes 49156
  211.2 4.3 %copy-start.7 = (f32[16,256]{1,0:T(8,128)S(1)}, f32[16,256]{1,0:T(8,128)}, u32[]{:S(2)}) copy-start(f32[16,256]{1,0:T(8,128)} %get-tuple-element.188) | copy-start | bytes 49156
  211.2 4.3 %copy-start.8 = (f32[16,256]{1,0:T(8,128)S(1)}, f32[16,256]{1,0:T(8,128)}, u32[]{:S(2)}) copy-start(f32[16,256]{1,0:T(8,128)} %get-tuple-element.192) | copy-start | bytes 49156
  211.2 4.3 %copy-start.9 = (f32[16,256]{1,0:T(8,128)S(1)}, f32[16,256]{1,0:T(8,128)}, u32[]{:S(2)}) copy-start(f32[16,256]{1,0:T(8,128)} %get-tuple-element.196) | copy-start | bytes 49156
  211.2 4.3 %copy-start.10 = (f32[16,256]{1,0:T(8,128)S(1)}, f32[16,256]{1,0:T(8,128)}, u32[]{:S(2)}) copy-start(f32[16,256]{1,0:T(8,128)} %get-tuple-element.200) | copy-start | bytes 49156
  211.2 4.3 %copy-start.11 = (f32[16,256]{1,0:T(8,128)S(1)}, f32[16,256]{1,0:T(8,128)}, u32[]{:S(2)}) copy-start(f32[16,256]{1,0:T(8,128)} %get-tuple-element.204) | copy-start | bytes 49156
  211.2 4.3 %copy-start.12 = (f32[16,256]{1,0:T(8,128)S(1)}, f32[16,256]{1,0:T(8,128)}, u32[]{:S(2)}) copy-start(f32[16,256]{1,0:T(8,128)} %get-tuple-element.208) | copy-start | bytes 49156
  211.2 4.3 %copy-start.13 = (f32[16,256]{1,0:T(8,128)S(1)}, f32[16,256]{1,0:T(8,128)}, u32[]{:S(2)}) copy-start(f32[16,256]{1,0:T(8,128)} %get-tuple-element.212) | copy-start | bytes 49156
  215.5 22.8 %slice-start = ((s8[7864320]{0:T(1024)(128)(4,1)}), s8[4194304]{0:T(1024)(128)(4,1)S(1)}, s32[]{:S(2)}) async-start(s8[7864320]{0:T(1024)(128)(4,1)} %bitcast.2758), calls=%async_computation.3 | async-start | bytes 8388608
  215.8 22.5 %slice-start.1 = ((s8[7864320]{0:T(1024)(128)(4,1)}), s8[3670016]{0:T(1024)(128)(4,1)S(1)}, s32[]{:S(2)}) async-start(s8[7864320]{0:T(1024)(128)(4,1)} %bitcast.2758), calls=%async_computation.4 | async-start | bytes 7340032
  215.8 22.5 %copy-start.35 = (f32[1,16,256]{2,1,0:T(8,128)S(1)}, f32[1,16,256]{2,1,0:T(8,128)}, u32[]{:S(2)}) copy-start(f32[1,16,256]{2,1,0:T(8,128)} %copy-done.34) | copy-start | bytes 49156
  215.8 22.5 %copy-start.37 = (f32[1,16,256]{2,1,0:T(8,128)S(1)}, f32[1,16,256]{2,1,0:T(8,128)}, u32[]{:S(2)}) copy-start(f32[1,16,256]{2,1,0:T(8,128)} %copy-done.36) | copy-start | bytes 49156
  215.8 22.5 %copy-start.39 = (f32[1,16,256]{2,1,0:T(8,128)S(1)}, f32[1,16,256]{2,1,0:T(8,128)}, u32[]{:S(2)}) copy-start(f32[1,16,256]{2,1,0:T(8,128)} %copy-done.38) | copy-start | bytes 49156
  215.8 22.5 %copy-start.41 = (f32[1,16,256]{2,1,0:T(8,128)S(1)}, f32[1,16,256]{2,1,0:T(8,128)}, u32[]{:S(2)}) copy-start(f32[1,16,256]{2,1,0:T(8,128)} %copy-done.40) | copy-start | bytes 49156
  215.8 22.5 %copy-start.43 = (f32[1,16,256]{2,1,0:T(8,128)S(1)}, f32[1,16,256]{2,1,0:T(8,128)}, u32[]{:S(2)}) copy-start(f32[1,16,256]{2,1,0:T(8,128)} %copy-done.42) | copy-start | bytes 49156
  215.8 22.5 %copy-start.54 = (f32[1,16,256]{2,1,0:T(8,128)S(1)}, f32[1,16,256]{2,1,0:T(8,128)}, u32[]{:S(2)}) copy-start(f32[1,16,256]{2,1,0:T(8,128)} %copy-done.53) | copy-start | bytes 49156
  244.5 39.4 %copy-start.21 = (f32[16,256]{1,0:T(8,128)S(1)}, f32[16,256]{1,0:T(8,128)}, u32[]{:S(2)}) copy-start(f32[16,256]{1,0:T(8,128)} %copy-done.19) | copy-start | bytes 49156
  283.9 26.4 %copy-start.91 = (s32[128,2]{0,1:T(2,128)S(1)}, s32[128,2]{0,1:T(2,128)}, u32[]{:S(2)}) copy-start(s32[128,2]{0,1:T(2,128)} %copy.53) | copy-start | bytes 3076
  309.3 39.0 %copy-start.90 = (s32[96]{0:T(128)S(1)}, s32[96]{0:T(128)}, u32[]{:S(2)}) copy-start(s32[96]{0:T(128)} %copy-done.89) | copy-start | bytes 1156
  348.3 15.0 %copy-start.1 = (f32[32,6,128]{2,0,1:T(8,128)S(1)}, f32[32,6,128]{2,0,1:T(8,128)}, u32[]{:S(2)}) copy-start(f32[32,6,128]{2,0,1:T(8,128)} %param.11) | copy-start | bytes 294916
  348.3 14.1 %copy-start.93 = (s32[96]{0:T(128)S(1)}, s32[96]{0:T(128)}, u32[]{:S(2)}) copy-start(s32[96]{0:T(128)} %param.13) | copy-start | bytes 1156
  (42 other events, 120.5 us)
where the time goes:
time: 368 us; the launch traced here: 363 us
  other arithmetic  145 us (39%)
  local copies, waits for them, and re-layouts  105 us (29%)
  starting transfers between devices  45.6 us (12%)
  blocking collectives  34.3 us (9%)
  matrix products  27.7 us (8%)
    unnamed x41, other arithmetic  42.3 us
    all_to_all x1, blocking collectives, shards(): lax.all_to_all(reply_rows.reshape(devices_all, slot_count, fields_num * t...  34.3 us
    unnamed x231, local copies, waits for them, and re-layouts  30.3 us
    slice x4, local copies, waits for them, and re-layouts, padded_2(): lax.slice_in_dim(block, 0, width, axis=dim)  29.1 us
    sub x1, other arithmetic, shards(): ocean_out = mixed_state - VISCOSITY * second_pass  25.4 us
    mul x1, other arithmetic, shards(): first_pass = wet_cells * laplace(with_rims(masked))  23.2 us
    mul x35, other arithmetic, thomas(): carried = value_list[k] - ratio_list[k][None] * carried  23 us
    concatenate x2, other arithmetic, padded_2(): block = jnp.concatenate([low, block, high], axis=dim)  18.5 us
  transfers between devices with their start and end apart: 10, of which 1 were waited for; matrix products, arithmetic and copies ran while one was open for 41% of the time, Pallas kernels for 0%

commit v1 on v0

v1 whole, which is shorter than its diff:
```python
import functools

import jax
import jax.numpy as jnp
from jax import lax
from jax.experimental import pallas as pl
from jax.experimental.pallas import tpu as pltpu
from jax.sharding import PartitionSpec as P

MESH = pl.DeviceIdType.MESH
F32 = jnp.float32
BF16 = jnp.bfloat16
VISCOSITY = 0.025
FORCING = 0.5
BACKGROUND = 0.05

DEVICES = 128
FIELDS = 6
LEVELS = 80
SLABS = LEVELS * FIELDS
ROWS = 16
COLS = 256
PAIRS = 96
BLOCKS = 32
STRIPS = 24
PITCH = 32
SENT = 25
GROUP = 64
GROUPS = 8
CHUNKS = 5
CHUNK_LEVELS = LEVELS // CHUNKS
CHUNK = SLABS // CHUNKS


def split2(v):
    hi = v.astype(BF16)
    lo = (v - hi.astype(F32)).astype(BF16)
    return hi, lo


def iota(shape, dim):
    return lax.broadcasted_iota(jnp.int32, shape, dim)


def column_square(dest_ref):
    column = jnp.concatenate([dest_ref[...], jnp.full((128 - PAIRS, 1), -1, jnp.int32)], axis=0)
    down = jnp.broadcast_to(column.astype(F32), (128, 128))
    return down, down.T


FLUX_STEP = 8


def flux_kernel(src_ref, weight_ref, flux_ref, dest_ref, block_ref, out_ref, parts, contrib):
    step = pl.program_id(0)

    @pl.when(step == 0)
    def _():
        contrib[...] = jnp.zeros_like(contrib)

        def prepare(b, carry):
            rows = jnp.concatenate([flux_ref[b], jnp.zeros((2, 128), F32)], axis=0)
            hi = rows.astype(BF16).astype(F32)
            both = jnp.concatenate([hi, rows - hi], axis=0).astype(BF16)
            parts[b] = jnp.concatenate([both, both], axis=1)
            return carry

        lax.fori_loop(0, BLOCKS, prepare, 0)

    for i in range(FLUX_STEP):
        g = step * FLUX_STEP + i
        left = parts[src_ref[g]]
        hi, lo = split2(weight_ref[i])
        right = jnp.concatenate([hi, lo], axis=0)
        both = jnp.dot(left, right, preferred_element_type=F32)
        value = both[:8] + both[8:]
        at = pl.multiple_of(g * 8, 8)
        contrib[pl.ds(at, 8), :] = value[:, :128]
        contrib[pl.ds(pl.multiple_of(1024 + g * 8, 8), 8), :] = value[:, 128:]

    @pl.when(step == pl.num_programs(0) - 1)
    def _():
        down, across = column_square(dest_ref)
        same = (down == across) & (iota((128, 128), 0) < iota((128, 128), 1))
        rank = jnp.sum(same.astype(F32), axis=0, keepdims=True)
        dest_here = across == iota((128, 128), 0).astype(F32)
        places = [dest_here & (rank == float(j)) for j in range(2)]
        rows = jnp.concatenate([block_ref[...].astype(F32), jnp.zeros((1, 128 - PAIRS), F32)], axis=1) + 1.0
        ids = [jnp.sum(jnp.where(p, rows, 0.0), axis=1, keepdims=True) - 1.0 for p in places]
        lane = iota((128, 128), 1)
        out_ref[pl.ds(STRIPS, 128, stride=PITCH), :] = jnp.where(lane == 0, ids[0], ids[1])
        place = jnp.concatenate([p.astype(F32).astype(BF16) for p in places], axis=0)
        place = jnp.concatenate([place, place], axis=1)
        for f in range(FIELDS):
            for h in range(2):
                hi, lo = split2(contrib[pl.ds(h * 1024 + f, 128, stride=8), :])
                got = jnp.dot(place, jnp.concatenate([hi, lo], axis=0), preferred_element_type=F32)
                for j in range(2):
                    out_ref[pl.ds(j * 12 + 2 * f + h, 128, stride=PITCH), :] = got[j * 128:(j + 1) * 128]


def flux_call(pair_weight, atm_flux, pair_src, pair_dest, pair_block):
    whole = lambda shape: pl.BlockSpec(shape, lambda i, s: (0,) * len(shape))
    return pl.pallas_call(
        flux_kernel,
        out_shape=jax.ShapeDtypeStruct((DEVICES * PITCH, 128), F32),
        grid_spec=pltpu.PrefetchScalarGridSpec(
            num_scalar_prefetch=1,
            grid=(PAIRS // FLUX_STEP,),
            in_specs=[
                pl.BlockSpec((FLUX_STEP, 128, COLS), lambda i, s: (i, 0, 0)),
                whole((BLOCKS, FIELDS, 128)),
                whole((PAIRS, 1)),
                whole((1, PAIRS)),
            ],
            out_specs=whole((DEVICES * PITCH, 128)),
            scratch_shapes=[
                pltpu.VMEM((BLOCKS, 16, 256), BF16),
                pltpu.VMEM((2048, 128), F32),
            ],
        ),
        compiler_params=pltpu.CompilerParams(vmem_limit_bytes=32 << 20),
        name="contributions",
    )(pair_src, pair_weight, atm_flux, pair_dest, pair_block.reshape(1, PAIRS))


def laplace(v):
    height, width = v.shape
    return (
        (pltpu.roll(v, height - 1, 0) + pltpu.roll(v, 1, 0))
        + (pltpu.roll(v, width - 1, 1) + pltpu.roll(v, 1, 1))
        - 4.0 * v
    )


def pack_columns(state, mask_ref, packed):
    lane = iota((ROWS, 128), 1)

    def group(g, carry):
        def one(j, acc):
            first, last = acc
            slab = jnp.minimum(g * GROUP + j, SLABS - 1)
            shift = 2 * j
            here = (lane == shift) | (lane == shift + 1)
            low = pltpu.roll(state[slab, :, :128], shift, 1)
            high = pltpu.roll(state[slab, :, 128:], lax.rem(shift + 2, 128), 1)
            return jnp.where(here, low, first), jnp.where(here, high, last)

        zero = jnp.zeros((ROWS, 128), F32)
        first, last = lax.fori_loop(0, GROUP, one, (zero, zero), unroll=4)
        packed[0, g] = first
        packed[1, g] = last
        return carry

    lax.fori_loop(0, GROUPS, group, 0)
    wet = mask_ref[...].astype(F32)
    g, shift = SLABS // GROUP, 2 * (SLABS % GROUP)
    here = (lane == shift) | (lane == shift + 1)
    packed[0, g] = jnp.where(here, pltpu.roll(wet[:, :128], shift, 1), packed[0, g])
    packed[1, g] = jnp.where(here, pltpu.roll(wet[:, 128:], shift + 2, 1), packed[1, g])


def side_columns(rim, slab):
    g = slab // GROUP
    shift = 2 * (slab - g * GROUP)
    right = pltpu.roll(rim[0, g], lax.rem(128 - shift, 128), 1)
    left = pltpu.roll(rim[1, g], 126 - shift, 1)
    return jnp.where(iota((24, 128), 1) < 64, right, left)


def coupling_at(k, depth, scale):
    kf = k.astype(F32)
    sigma = (kf + 1.0) / depth
    rest = 1.0 - sigma
    profile = BACKGROUND + 6.75 * sigma * rest * rest
    value = scale * jnp.where(kf < depth, profile, BACKGROUND)
    return jnp.where(k >= 0, value, 0.0)


def sweep_up(state, mask_ref, depth_ref, scale_ref, value, ratio, first_inverse):
    for half in range(2):
        rows = pl.ds(8 * half, 8)
        wet = mask_ref[rows, :].astype(F32)
        depth = depth_ref[rows, :].astype(F32)
        scale = scale_ref[rows, :]

        def level(i, carry):
            below, open_now, values = carry
            k = LEVELS - 1 - i
            above = coupling_at(k - 1, depth, scale)
            inverse = 1.0 / (1.0 + above + below * open_now)
            ratio_now = above * inverse
            ratio[k, rows, :] = ratio_now
            weight = below * inverse
            wet_inverse = wet * inverse
            new = []
            for f in range(FIELDS):
                now = wet_inverse * state[k * FIELDS + f, rows, :] + weight * values[f]
                value[k * FIELDS + f, rows, :] = now
                new.append(now)

            @pl.when(k == 0)
            def _():
                first_inverse[rows, :] = inverse

            return above, 1.0 - ratio_now, tuple(new)

        zero = jnp.zeros((8, COLS), F32)
        lax.fori_loop(0, LEVELS, level, (zero, zero, (zero,) * FIELDS))


def ocean_level(k, state, rims, rim, wet_wide, value, ratio, response, previous):
    ratio_now = ratio[k]
    response[k] = jnp.where(k == 0, response[k], ratio_now * response[jnp.maximum(k - 1, 0)])
    for f in range(FIELDS):
        slab = k * FIELDS + f
        tall = jnp.concatenate([state[slab], rims[slab]], axis=0)
        wide = jnp.concatenate([tall, side_columns(rim, slab)], axis=1)
        first = wet_wide[...] * laplace(wet_wide[...] * wide)
        second = wet_wide[:ROWS, :COLS] * laplace(first)[:ROWS, :COLS]
        mixed = value[slab] + ratio_now * previous[f]
        previous[f] = mixed
        value[slab] = mixed - VISCOSITY * second


def exchange_kernel(
    out_hbm, state_hbm, mask_ref, depth_ref, scale_ref,
    base_hbm, response, forced, answered,
    state, value, ratio, rims, mask_rims, packed, rim, wet_wide, previous, arrived, reply,
    load_sem, store_sem, send_sem, recv_sem, own_sem, row_send, row_recv, edge_send, edge_recv,
):
    ox, oy = lax.axis_index("ox"), lax.axis_index("oy")
    me = ox * 8 + oy
    loads = []
    for c in range(CHUNKS):
        at = pl.ds(c * CHUNK, CHUNK)
        loads.append(pltpu.make_async_copy(state_hbm.at[at], state.at[at], load_sem.at[c]))
        loads[-1].start()

    barrier = pltpu.get_barrier_semaphore()

    def partner(k):
        t = lax.rem(me + k, DEVICES)
        return t, (t // 8, lax.rem(t, 8))

    def greet(k, carry):
        pl.semaphore_signal(barrier, inc=1, device_id=partner(k)[1], device_id_type=MESH)
        return carry

    rim[...] = jnp.zeros_like(rim)
    previous[...] = jnp.zeros_like(previous)
    lax.fori_loop(1, DEVICES, greet, 0)
    pl.semaphore_wait(barrier, DEVICES - 1)

    def to_all(source, target, count, i):
        def send(k, carry):
            t, device = partner(k)
            pltpu.make_async_remote_copy(
                source.at[pl.ds(pl.multiple_of(t * PITCH, PITCH), count)],
                target.at[pl.ds(pl.multiple_of(me * PITCH, PITCH), count)],
                send_sem.at[i], recv_sem.at[i], device_id=device, device_id_type=MESH,
            ).start()
            return carry

        lax.fori_loop(1, DEVICES, send, 0)
        mine = pl.ds(pl.multiple_of(me * PITCH, PITCH), count)
        own = pltpu.make_async_copy(source.at[mine], target.at[mine], own_sem.at[i])
        own.start()
        return own

    def finish(source, target, count, i, own):
        rows = pl.ds(0, (DEVICES - 1) * count)
        pltpu.make_async_copy(source.at[rows], target.at[rows], send_sem.at[i]).wait()
        pltpu.make_async_copy(source.at[rows], target.at[rows], recv_sem.at[i]).wait()
        own.wait()

    own = to_all(out_hbm, arrived, SENT, 0)

    up, down = lax.rem(ox + 15, 16), lax.rem(ox + 1, 16)
    back, ahead = lax.rem(oy + 7, 8), lax.rem(oy + 1, 8)
    row_copies = []
    for c in range(CHUNKS):
        at = pl.ds(c * CHUNK, CHUNK)
        for d, (mine, there, device) in enumerate(((14, 6, down), (0, 0, up))):
            copy = pltpu.make_async_remote_copy(
                state_hbm.at[at, pl.ds(mine, 2)], rims.at[at, pl.ds(there, 2)],
                row_send.at[c, d], row_recv.at[c, d], device_id=(device, oy), device_id_type=MESH,
            )
            copy.start()
            row_copies.append(copy)
    edge_copies = []

    def edge(source, target, device):
        n = len(edge_copies)
        copy = pltpu.make_async_remote_copy(
            source, target, edge_send.at[n], edge_recv.at[n], device_id=device, device_id_type=MESH
        )
        copy.start()
        edge_copies.append(copy)

    edge(mask_ref.at[pl.ds(8, 8)], mask_rims.at[0], (down, oy))
    edge(mask_ref.at[pl.ds(0, 8)], mask_rims.at[1], (up, oy))

    for load in loads:
        load.wait()
    pack_columns(state, mask_ref, packed)
    for side, y in ((0, back), (1, ahead)):
        edge(packed.at[side], rim.at[side, :, pl.ds(0, ROWS)], (ox, y))
        edge(packed.at[side, :, pl.ds(0, 1)], rim.at[side, :, pl.ds(16, 1)], (up, y))
        edge(packed.at[side, :, pl.ds(15, 1)], rim.at[side, :, pl.ds(23, 1)], (down, y))

    sweep_up(state, mask_ref, depth_ref, scale_ref, value, ratio, response.at[0])

    for copy in edge_copies:
        copy.wait()
    wet = mask_ref[...].astype(F32)
    row8 = iota((8, COLS), 0)
    below = mask_rims[1].astype(F32) * (ox < 15).astype(F32)
    above = mask_rims[0].astype(F32) * (ox > 0).astype(F32)
    tall = jnp.concatenate([wet, jnp.where(row8 < 4, below, above)], axis=0)
    side = side_columns(rim, SLABS)
    lane = iota((24, 128), 1)
    row = iota((24, 128), 0)
    ok = jnp.where(lane < 64, (oy < 7).astype(F32), (oy > 0).astype(F32))
    ok = ok * jnp.where(row < 16, 1.0, jnp.where(row < 20, (ox < 15).astype(F32), (ox > 0).astype(F32)))
    wet_wide[...] = jnp.concatenate([tall, side * ok], axis=1)
    for copy in row_copies[:2]:
        copy.wait()
    level = functools.partial(
        ocean_level, state=state, rims=rims, rim=rim, wet_wide=wet_wide, value=value, ratio=ratio,
        response=response, previous=previous,
    )
    level(jnp.int32(0))

    finish(out_hbm, arrived, SENT, 0, own)
    ids = arrived[pl.ds(STRIPS, 128, stride=PITCH), :]
    ids = jnp.concatenate([ids[:, 0:1], ids[:, 1:2]], axis=0)
    lane = iota((256, 128), 1)
    hit = (ids == (lane & 15).astype(F32)) & (lane < 48)
    spread = hit.astype(F32)
    gather = spread.T[:ROWS].astype(BF16)
    spread = spread.astype(BF16)
    for f in range(FIELDS):
        for h in range(2):
            lanes = pl.ds(128 * h, 128)
            strip = 2 * f + h
            got = jnp.concatenate(
                [arrived[pl.ds(j * 12 + strip, 128, stride=PITCH), :] for j in range(2)], axis=0
            )
            hi, lo = split2(got)
            flux = jnp.dot(gather, hi, preferred_element_type=F32) + jnp.dot(gather, lo, preferred_element_type=F32)
            forcing = FORCING * mask_ref[:, lanes].astype(F32) * flux
            forced[f, :, lanes] = forcing
            surface = value[f, :, lanes] + response[0, :, lanes] * forcing
            top = surface.astype(BF16)
            rest = surface - top.astype(F32)
            middle = rest.astype(BF16)
            last = (rest - middle.astype(F32)).astype(BF16)
            right = jnp.concatenate([top, middle, last, jnp.zeros((80, 128), BF16)], axis=0)
            back_rows = jnp.dot(spread, right, preferred_element_type=F32)
            for j in range(2):
                reply[pl.ds(j * 12 + strip, 128, stride=PITCH), :] = back_rows[j * 128:(j + 1) * 128]
    own = to_all(reply, answered, STRIPS, 1)

    stores = []
    for c in range(CHUNKS):
        if c > 0:
            for copy in row_copies[2 * c:2 * c + 2]:
                copy.wait()

        def step(k, carry):
            level(k)
            return carry

        lax.fori_loop(max(1, c * CHUNK_LEVELS), (c + 1) * CHUNK_LEVELS, step, 0)
        at = pl.ds(c * CHUNK, CHUNK)
        stores.append(pltpu.make_async_copy(value.at[at], base_hbm.at[at], store_sem.at[c]))
        stores[-1].start()
    finish(reply, answered, STRIPS, 1, own)
    for store in stores:
        store.wait()


def exchange_call(outgoing, state, mask, depth, scale):
    vmem = pl.BlockSpec(memory_space=pltpu.VMEM)
    anywhere = pl.BlockSpec(memory_space=pl.ANY)
    dma = pltpu.SemaphoreType.DMA
    return pl.pallas_call(
        exchange_kernel,
        out_shape=(
            jax.ShapeDtypeStruct((SLABS, ROWS, COLS), F32),
            jax.ShapeDtypeStruct((LEVELS, ROWS, COLS), F32),
            jax.ShapeDtypeStruct((FIELDS, ROWS, COLS), F32),
            jax.ShapeDtypeStruct((DEVICES * PITCH, 128), F32),
        ),
        in_specs=[anywhere, anywhere, vmem, vmem, vmem],
        out_specs=(anywhere, vmem, vmem, vmem),
        scratch_shapes=[
            pltpu.VMEM((SLABS, ROWS, COLS), F32),
            pltpu.VMEM((SLABS, ROWS, COLS), F32),
            pltpu.VMEM((LEVELS, ROWS, COLS), F32),
            pltpu.VMEM((SLABS, 8, COLS), F32),
            pltpu.VMEM((2, 8, COLS), jnp.int32),
            pltpu.VMEM((2, GROUPS, ROWS, 128), F32),
            pltpu.VMEM((2, GROUPS, 24, 128), F32),
            pltpu.VMEM((24, 384), F32),
            pltpu.VMEM((FIELDS, ROWS, COLS), F32),
            pltpu.VMEM((DEVICES * PITCH, 128), F32),
            pltpu.VMEM((DEVICES * PITCH, 128), F32),
            dma((CHUNKS,)), dma((CHUNKS,)), dma((2,)), dma((2,)), dma((2,)),
            dma((CHUNKS, 2)), dma((CHUNKS, 2)), dma((8,)), dma((8,)),
        ],
        compiler_params=pltpu.CompilerParams(
            collective_id=0, has_side_effects=True, vmem_limit_bytes=50 << 20
        ),
        name="exchange",
    )(outgoing, state, mask, depth, scale)


LAST_STEPS = 16
LAST_PAIRS = PAIRS // LAST_STEPS
LAST_LEVELS = LEVELS // LAST_STEPS


def last_kernel(src_ref, weight_ref, base_ref, response_ref, forced_ref, answered_ref, dest_ref,
                ocean_ref, surface_ref, rows, total):
    step = pl.program_id(0)

    @pl.when(step == 0)
    def _():
        total[...] = jnp.zeros_like(total)
        rows[...] = jnp.zeros_like(rows)
        down, across = column_square(dest_ref)
        same = (down == across) & (iota((128, 128), 1) < iota((128, 128), 0))
        rank = jnp.sum(same.astype(F32), axis=1, keepdims=True)
        dest_here = down == iota((128, 128), 1).astype(F32)
        pick = jnp.concatenate(
            [(dest_here & (rank == float(j))).astype(F32).astype(BF16) for j in range(2)], axis=1
        )
        for f in range(FIELDS):
            for h in range(2):
                got = jnp.concatenate(
                    [answered_ref[pl.ds(j * 12 + 2 * f + h, 128, stride=PITCH), :] for j in range(2)], axis=0
                )
                hi, lo = split2(got)
                rows[pl.ds(h * 1024 + f, 128, stride=8), :] = (
                    jnp.dot(pick, hi, preferred_element_type=F32) + jnp.dot(pick, lo, preferred_element_type=F32)
                )

    for k in range(LAST_LEVELS):
        for f in range(FIELDS):
            ocean_ref[k * FIELDS + f] = base_ref[k * FIELDS + f] + response_ref[k] * forced_ref[f]

    for i in range(LAST_PAIRS):
        g = step * LAST_PAIRS + i
        row = jnp.concatenate(
            [rows[pl.ds(pl.multiple_of(h * 1024 + g * 8, 8), 8), :] for h in range(2)], axis=1
        )
        hi = row.astype(BF16).astype(F32)
        left = jnp.concatenate([hi, row - hi], axis=0).astype(BF16)
        top, low = split2(weight_ref[i])
        right = jnp.concatenate([top, low], axis=0)
        both = lax.dot_general(left, right, (((1,), (1,)), ((), ())), preferred_element_type=F32)
        both = both[:8] + both[8:]
        at = src_ref[g]
        total[at] = total[at] + both[:, :128] + both[:, 128:]

    @pl.when(step == LAST_STEPS - 1)
    def _():
        surface_ref[...] = total[:, :FIELDS, :]


def last_call(pair_weight, base, response, forced, answered, pair_src, pair_dest):
    whole = lambda shape: pl.BlockSpec(shape, lambda i, s: (0,) * len(shape))
    part = LAST_LEVELS * FIELDS
    return pl.pallas_call(
        last_kernel,
        out_shape=(
            jax.ShapeDtypeStruct((SLABS, ROWS, COLS), F32),
            jax.ShapeDtypeStruct((BLOCKS, FIELDS, 128), F32),
        ),
        grid_spec=pltpu.PrefetchScalarGridSpec(
            num_scalar_prefetch=1,
            grid=(LAST_STEPS,),
            in_specs=[
                pl.BlockSpec((LAST_PAIRS, 128, COLS), lambda i, s: (i, 0, 0)),
                pl.BlockSpec((part, ROWS, COLS), lambda i, s: (i, 0, 0)),
                pl.BlockSpec((LAST_LEVELS, ROWS, COLS), lambda i, s: (i, 0, 0)),
                whole((FIELDS, ROWS, COLS)),
                whole((DEVICES * PITCH, 128)),
                whole((PAIRS, 1)),
            ],
            out_specs=(
                pl.BlockSpec((part, ROWS, COLS), lambda i, s: (i, 0, 0)),
                whole((BLOCKS, FIELDS, 128)),
            ),
            scratch_shapes=[
                pltpu.VMEM((2048, 128), F32),
                pltpu.VMEM((BLOCKS, 8, 128), F32),
            ],
        ),
        compiler_params=pltpu.CompilerParams(vmem_limit_bytes=40 << 20),
        name="outputs",
    )(pair_src, pair_weight, base, response, forced, answered, pair_dest)


def shards(atm_flux, pair_weight, pair_src, pair_dest, pair_block, ocean_state, land_mask, kpp_depth, mixing_scale):
    outgoing = flux_call(pair_weight, atm_flux, pair_src, pair_dest, pair_block)
    state = ocean_state.reshape(SLABS, ROWS, COLS)
    base, response, forced, answered = exchange_call(outgoing, state, land_mask, kpp_depth, mixing_scale)
    ocean, surface = last_call(pair_weight, base, response, forced, answered, pair_src, pair_dest)
    return ocean.reshape(LEVELS, FIELDS, ROWS, COLS), surface


def solution(mesh):
    return jax.shard_map(
        shards,
        mesh=mesh,
        in_specs=(
            P(("ox", "oy"), None, None),
            P(("ox", "oy"), None, None),
            P(("ox", "oy")),
            P(("ox", "oy"), None),
            P(("ox", "oy")),
            P(None, None, "ox", "oy"),
            P("ox", "oy"),
            P("ox", "oy"),
            P("ox", "oy"),
        ),
        out_specs=(P(None, None, "ox", "oy"), P(("ox", "oy"), None, None)),
        check_vma=False,
    )
```

time: 368 us -> 135 us (0.37)
  other arithmetic: 145 us -> 0 us
  Pallas kernels: 0 us -> 121 us
  local copies, waits for them, and re-layouts: 105 us -> 12.8 us
  starting transfers between devices: 45.6 us -> 0 us
  blocking collectives: 34.3 us -> 0 us
  matrix products: 27.7 us -> 0 us
    pallas_call x0 -> x3, Pallas kernels: none -> 121 us  [the longest x1 97.8 us: exchange_call(): pl.pallas_call(exchange_kernel, out_shape=(jax.ShapeDtypeStruct((SLABS, R...]
    mul x42 -> x0, other arithmetic: 54 us -> none  [the longest x1 23.2 us: shards(): first_pass = wet_cells * laplace(with_rims(masked))]
    slice x8 -> x0, local copies, waits for them, and re-layouts: 44.5 us -> none  [the longest x4 29.1 us: padded_2(): lax.slice_in_dim(block, 0, width, axis=dim)]
    unnamed x41 -> x0, other arithmetic: 42.3 us -> none
    all_to_all x1 -> x0, blocking collectives: 34.3 us -> none  [shards(): lax.all_to_all(reply_rows.reshape(devices_all, slot_count, fields_num * t...]
    dot_general x8 -> x0, matrix products: 27.7 us -> none  [the longest x1 13.1 us: shards(): jnp.einsum('gfo,gao->gfa', per_pair, pair_weight, precision=HIGHEST)]
    sub x2 -> x0, other arithmetic: 25.4 us -> none  [the longest x1 25.4 us: shards(): ocean_out = mixed_state - VISCOSITY * second_pass]
    all_to_all x2 -> x0, starting transfers between devices: 23.3 us -> none  [the longest x1 12 us: shards(): lax.all_to_all(outgoing_ids.reshape(devices_all, slot_count), ('ox', 'oy'...]
  transfers between devices with their start and end apart: 10 -> 0, of which waited for: 1 -> 0; matrix products, arithmetic and copies ran while one was open for 41% -> 0% of each run, Pallas kernels for 0% -> 0%
where the time goes in v1:
time: 135 us; the launch traced here: 134 us
  Pallas kernels  121 us (90%)
  local copies, waits for them, and re-layouts  12.8 us (9%)
    pallas_call x1, Pallas kernels, exchange_call(): pl.pallas_call(exchange_kernel, out_shape=(jax.ShapeDtypeStruct((SLABS, R...  97.8 us
    pallas_call x1, Pallas kernels, last_call(): pl.pallas_call(last_kernel, out_shape=(jax.ShapeDtypeStruct((SLABS, ROWS,...  17.1 us
    unnamed x21, local copies, waits for them, and re-layouts  12.8 us
    pallas_call x1, Pallas kernels, flux_call(): pl.pallas_call(flux_kernel, out_shape=jax.ShapeDtypeStruct((DEVICES * PIT...  5.65 us

profile of v1, /device:TPU:1, one launch (start us, length us, event | category | flops | bytes accessed | tf_op | source)
XLA Modules:
  0.0 134.1 jit_solution(11247330257543553085)
XLA Ops:
  0.6 0.0 copy-start.5
  0.6 0.0 copy-start.4
  0.7 0.0 copy-start.3
  0.7 0.8 copy.12.dest_ref
  1.4 1.0 copy.11.flux_ref
  2.4 0.0 copy-start
  2.4 4.6 %copy-done = f32[96,128,256]{2,1,0:T(8,128)S(1)} copy-done((f32[96,128,256]{2,1,0:T(8,128)S(1)}, f32[96,128,256]{2,1,0:T(8,128)}, u32[]{:S(2)}) %copy-start) | copy-done | bytes 12582936
  7.0 0.0 copy-start.6
  7.0 0.7 copy-done.6
  7.6 0.0 copy-start.8
  7.6 0.7 copy-done.8
  8.3 5.7 %contributions.1.out_hbm = f32[4096,128]{1,0:T(8,128)S(1)} custom-call(s32[96]{0:T(128)S(1)} %copy-done.6, f32[96,128,256]{2,1,0:T(8,128)S(1)} %copy-done, f32[32,6,128]{2,1,0:T(8,128)S(1)} %copy.11.flux_ref, s32[96,1]{1,0:T(8,128)S(1)} %copy.12.dest_ref, s32[1,96]{1,0:T(1,128)S(1)} %bitcast.3), custom_call_target="tpu_custom_call" | custom-call | tf_op jit(solution)/shard_map/contributions/pallas_call | solution.py:104
  13.9 0.0 copy-start.1
  14.0 1.3 copy-done.1
  15.3 0.0 copy-done.5
  15.3 0.0 copy-done.4
  15.3 0.0 copy-done.3
  15.3 0.0 copy-start.7
  15.3 97.8 %exchange.1 = (f32[480,16,256]{2,1,0:T(8,128)}, f32[80,16,256]{2,1,0:T(8,128)S(1)}, f32[6,16,256]{2,1,0:T(8,128)S(1)}, f32[4096,128]{1,0:T(8,128)S(1)}) custom-call(f32[4096,128]{1,0:T(8,128)} %copy-done.1, f32[480,16,256]{2,1,0:T(8,128)} %bitcast.4, s32[16,256]{1,0:T(8,128)S(1)} %copy-done.3, s32[16,256]{1,0:T(8,128)S(1)} %copy-done.4, f32[16,256]{1,0:T(8,128)S(1)} %copy-done.5), custom_call_target="tpu_custom_call" | custom-call | tf_op jit(solution)/shard_map/exchange/pallas_call | solution.py:388
  113.1 0.0 copy-done.7
  113.1 0.0 copy-start.2
  113.1 3.2 %copy-done.2 = f32[480,16,256]{2,1,0:T(8,128)S(1)} copy-done((f32[480,16,256]{2,1,0:T(8,128)S(1)}, f32[480,16,256]{2,1,0:T(8,128)}, u32[]{:S(2)}) %copy-start.2) | copy-done | bytes 7864344
  116.3 17.1 %outputs.1 = (f32[480,16,256]{2,1,0:T(8,128)}, f32[32,6,128]{2,1,0:T(8,128)S(1)}) custom-call(s32[96]{0:T(128)S(1)} %copy-done.7, f32[96,128,256]{2,1,0:T(8,128)} %weight_ref.3, f32[480,16,256]{2,1,0:T(8,128)S(1)} %copy-done.2, f32[80,16,256]{2,1,0:T(8,128)S(1)} %get-tuple-element.9.response_ref, f32[6,16,256]{2,1,0:T(8,128)S(1)} %get-tuple-element.10.forced_ref, ...), custom_call_target="tpu_custom_call" | custom-call | tf_op jit(solution)/shard_map/outputs/pallas_call | solution.py:476
  133.5 0.7 copy.14
Async XLA Ops:
  0.6 14.6 %copy-start.5 = (f32[16,256]{1,0:T(8,128)S(1)}, f32[16,256]{1,0:T(8,128)}, u32[]{:S(2)}) copy-start(f32[16,256]{1,0:T(8,128)} %scale_ref.1) | copy-start | bytes 49156
  0.6 14.6 %copy-start.4 = (s32[16,256]{1,0:T(8,128)S(1)}, s32[16,256]{1,0:T(8,128)}, u32[]{:S(2)}) copy-start(s32[16,256]{1,0:T(8,128)} %depth_ref.1) | copy-start | bytes 49156
  0.7 14.6 %copy-start.3 = (s32[16,256]{1,0:T(8,128)S(1)}, s32[16,256]{1,0:T(8,128)}, u32[]{:S(2)}) copy-start(s32[16,256]{1,0:T(8,128)} %mask_ref.1) | copy-start | bytes 49156
  2.4 4.6 %copy-start = (f32[96,128,256]{2,1,0:T(8,128)S(1)}, f32[96,128,256]{2,1,0:T(8,128)}, u32[]{:S(2)}) copy-start(f32[96,128,256]{2,1,0:T(8,128)} %weight_ref.3) | copy-start | bytes 37748740
  7.0 0.7 copy-start.6
  7.6 0.7 copy-start.8
  13.9 1.3 copy-start.1
  15.3 97.8 %copy-start.7 = (s32[96]{0:T(128)S(1)}, s32[96]{0:T(128)}, u32[]{:S(2)}) copy-start(s32[96]{0:T(128)} %src_ref.3) | copy-start | bytes 1156
  113.1 3.2 %copy-start.2 = (f32[480,16,256]{2,1,0:T(8,128)S(1)}, f32[480,16,256]{2,1,0:T(8,128)}, u32[]{:S(2)}) copy-start(f32[480,16,256]{2,1,0:T(8,128)} %get-tuple-element.8.base_ref) | copy-start | bytes 23592964

commit v2 on v1

--- a/solution.py
+++ b/solution.py
@@ -28,6 +28,10 @@
 GROUP = 64
 GROUPS = 8
 CHUNKS = 5
+EARLY = 2
+BATCH = 4
+LIMIT_R = 54
+LIMIT_L = 58
 CHUNK_LEVELS = LEVELS // CHUNKS
 CHUNK = SLABS // CHUNKS
 
@@ -42,24 +46,31 @@
     return lax.broadcasted_iota(jnp.int32, shape, dim)
 
 
-def column_square(dest_ref):
-    column = jnp.concatenate([dest_ref[...], jnp.full((128 - PAIRS, 1), -1, jnp.int32)], axis=0)
-    down = jnp.broadcast_to(column.astype(F32), (128, 128))
-    return down, down.T
+def row_square(dest_ref):
+    row = jnp.concatenate([dest_ref[...], jnp.full((1, 128 - PAIRS), -1, jnp.int32)], axis=1)
+    across = jnp.broadcast_to(row.astype(F32), (128, 128))
+    return across.T, across
 
 
 FLUX_STEP = 8
 
 
-def flux_kernel(src_ref, weight_ref, flux_ref, dest_ref, block_ref, out_ref, parts, contrib):
+def part_copy(weight_hbm, weights, sem, i, count):
+    at = pl.ds(i * count, count)
+    return pltpu.make_async_copy(weight_hbm.at[at], weights.at[at], sem.at[i])
+
+
+def flux_kernel(src_ref, weight_hbm, flux_ref, dest_ref, block_ref, out_ref, parts, contrib, weights, sem):
     step = pl.program_id(0)
 
     @pl.when(step == 0)
     def _():
+        for i in range(PAIRS // FLUX_STEP):
+            part_copy(weight_hbm, weights, sem, i, FLUX_STEP).start()
         contrib[...] = jnp.zeros_like(contrib)
 
         def prepare(b, carry):
-            rows = jnp.concatenate([flux_ref[b], jnp.zeros((2, 128), F32)], axis=0)
+            rows = jnp.concatenate([flux_ref[:, b, :], jnp.zeros((2, 128), F32)], axis=0)
             hi = rows.astype(BF16).astype(F32)
             both = jnp.concatenate([hi, rows - hi], axis=0).astype(BF16)
             parts[b] = jnp.concatenate([both, both], axis=1)
@@ -67,10 +78,11 @@
 
         lax.fori_loop(0, BLOCKS, prepare, 0)
 
+    part_copy(weight_hbm, weights, sem, step, FLUX_STEP).wait()
     for i in range(FLUX_STEP):
         g = step * FLUX_STEP + i
         left = parts[src_ref[g]]
-        hi, lo = split2(weight_ref[i])
+        hi, lo = split2(weights[g])
         right = jnp.concatenate([hi, lo], axis=0)
         both = jnp.dot(left, right, preferred_element_type=F32)
         value = both[:8] + both[8:]
@@ -80,7 +92,7 @@
 
     @pl.when(step == pl.num_programs(0) - 1)
     def _():
-        down, across = column_square(dest_ref)
+        down, across = row_square(dest_ref)
         same = (down == across) & (iota((128, 128), 0) < iota((128, 128), 1))
         rank = jnp.sum(same.astype(F32), axis=0, keepdims=True)
         dest_here = across == iota((128, 128), 0).astype(F32)
@@ -108,48 +120,42 @@
             num_scalar_prefetch=1,
             grid=(PAIRS // FLUX_STEP,),
             in_specs=[
-                pl.BlockSpec((FLUX_STEP, 128, COLS), lambda i, s: (i, 0, 0)),
-                whole((BLOCKS, FIELDS, 128)),
-                whole((PAIRS, 1)),
+                pl.BlockSpec(memory_space=pl.ANY),
+                whole((FIELDS, BLOCKS, 128)),
+                whole((1, PAIRS)),
                 whole((1, PAIRS)),
             ],
             out_specs=whole((DEVICES * PITCH, 128)),
             scratch_shapes=[
                 pltpu.VMEM((BLOCKS, 16, 256), BF16),
                 pltpu.VMEM((2048, 128), F32),
+                pltpu.VMEM((PAIRS, 128, COLS), F32),
+                pltpu.SemaphoreType.DMA((PAIRS // FLUX_STEP,)),
             ],
         ),
-        compiler_params=pltpu.CompilerParams(vmem_limit_bytes=32 << 20),
+        compiler_params=pltpu.CompilerParams(vmem_limit_bytes=56 << 20),
         name="contributions",
-    )(pair_src, pair_weight, atm_flux, pair_dest, pair_block.reshape(1, PAIRS))
-
-
-def laplace(v):
-    height, width = v.shape
-    return (
-        (pltpu.roll(v, height - 1, 0) + pltpu.roll(v, 1, 0))
-        + (pltpu.roll(v, width - 1, 1) + pltpu.roll(v, 1, 1))
-        - 4.0 * v
-    )
+    )(pair_src, pair_weight, jnp.transpose(atm_flux, (1, 0, 2)), pair_dest.reshape(1, PAIRS), pair_block.reshape(1, PAIRS))
 
 
 def pack_columns(state, mask_ref, packed):
     lane = iota((ROWS, 128), 1)
 
     def group(g, carry):
-        def one(j, acc):
-            first, last = acc
+        first = jnp.zeros((ROWS, 128), F32)
+        last = jnp.zeros((ROWS, 128), F32)
+        for j in range(GROUP):
             slab = jnp.minimum(g * GROUP + j, SLABS - 1)
-            shift = 2 * j
-            here = (lane == shift) | (lane == shift + 1)
-            low = pltpu.roll(state[slab, :, :128], shift, 1)
-            high = pltpu.roll(state[slab, :, 128:], lax.rem(shift + 2, 128), 1)
-            return jnp.where(here, low, first), jnp.where(here, high, last)
-
-        zero = jnp.zeros((ROWS, 128), F32)
-        first, last = lax.fori_loop(0, GROUP, one, (zero, zero), unroll=4)
+            both = jnp.where(lane < 64, state[slab, :, :128], state[slab, :, 128:])
+            if j:
+                both = pltpu.roll(both, 2 * j, 1)
+            first = jnp.where(lane >= 2 * j, both, first)
+            if j == 0:
+                last = both
+            else:
+                last = jnp.where((lane >= 2 * j - 2) & (lane < 126), both, last)
         packed[0, g] = first
-        packed[1, g] = last
+        packed[1, g] = pltpu.roll(last, 2, 1)
         return carry
 
     lax.fori_loop(0, GROUPS, group, 0)
@@ -160,12 +166,35 @@
     packed[1, g] = jnp.where(here, pltpu.roll(wet[:, 128:], shift + 2, 1), packed[1, g])
 
 
-def side_columns(rim, slab):
-    g = slab // GROUP
-    shift = 2 * (slab - g * GROUP)
-    right = pltpu.roll(rim[0, g], lax.rem(128 - shift, 128), 1)
-    left = pltpu.roll(rim[1, g], 126 - shift, 1)
-    return jnp.where(iota((24, 128), 1) < 64, right, left)
+def side_setup(packed, rim, side_mask, side_state, side_first):
+    at, here = SLABS // GROUP, 2 * (SLABS % GROUP)
+
+    def wet_of(block):
+        rows = block.shape[0]
+        even = (iota((rows, 128), 1) & 1) == 0
+        return jnp.where(even, block[:, here:here + 1], block[:, here + 1:here + 2])
+
+    wets = [wet_of(rim[s, at]) * side_mask[s] for s in range(2)]
+    owns = [wet_of(packed[s, at]) for s in range(2)]
+    even = (iota((24, 128), 1) & 1) == 0
+
+    def group(g, carry):
+        right, left = wets[0] * rim[0, g], wets[1] * rim[1, g]
+        side_state[g] = jnp.where(even, right, left)
+        own_low, own_high = owns[0] * packed[0, g], owns[1] * packed[1, g]
+        tall = lambda v: (pltpu.roll(v, 23, 0) + pltpu.roll(v, 1, 0) - 4.0 * v)[:ROWS]
+        first_right = wets[0][:ROWS] * (tall(right) + pltpu.roll(right[:ROWS] + own_high, 127, 1))
+        first_left = wets[1][:ROWS] * (tall(left) + pltpu.roll(left[:ROWS] + own_low, 1, 1))
+        side_first[g] = jnp.where(even[:ROWS], first_right, first_left)
+        return carry
+
+    lax.fori_loop(0, GROUPS, group, 0)
+
+
+def split_rows(parts):
+    whole = jnp.concatenate(parts, axis=0)
+    rest = whole - whole.astype(BF16).astype(F32)
+    return jnp.concatenate([whole, rest], axis=0).astype(BF16)
 
 
 def coupling_at(k, depth, scale):
@@ -209,25 +238,48 @@
         lax.fori_loop(0, LEVELS, level, (zero, zero, (zero,) * FIELDS))
 
 
-def ocean_level(k, state, rims, rim, wet_wide, value, ratio, response, previous):
-    ratio_now = ratio[k]
-    response[k] = jnp.where(k == 0, response[k], ratio_now * response[jnp.maximum(k - 1, 0)])
-    for f in range(FIELDS):
-        slab = k * FIELDS + f
-        tall = jnp.concatenate([state[slab], rims[slab]], axis=0)
-        wide = jnp.concatenate([tall, side_columns(rim, slab)], axis=1)
-        first = wet_wide[...] * laplace(wet_wide[...] * wide)
-        second = wet_wide[:ROWS, :COLS] * laplace(first)[:ROWS, :COLS]
-        mixed = value[slab] + ratio_now * previous[f]
-        previous[f] = mixed
-        value[slab] = mixed - VISCOSITY * second
+def ocean_levels(k, state, rims, side_state, side_first, wet_tall, along, value, ratio, response, previous):
+    wet = wet_tall[...]
+    count = BATCH * FIELDS
+    start = k * FIELDS
+
+    def sides(source, slab, rows):
+        g = slab // GROUP
+        values = pltpu.roll(source[g], 127 - 2 * (slab - g * GROUP), 1)
+        lane = iota((rows, 128), 1)
+        return jnp.concatenate([jnp.where(lane == 0, values, 0.0), jnp.where(lane == 127, values, 0.0)], axis=1)
+
+    masked = [wet * jnp.concatenate([state[start + i], rims[start + i]], axis=0) for i in range(count)]
+    cross = jnp.dot(split_rows(masked), along[...], preferred_element_type=F32)
+    firsts = []
+    for i in range(count):
+        v = masked[i]
+        straight = cross[24 * i:24 * i + 24] + cross[24 * (count + i):24 * (count + i) + 24]
+        total = (pltpu.roll(v, 23, 0) + pltpu.roll(v, 1, 0)) + (straight + sides(side_state, start + i, 24))
+        firsts.append(wet * total)
+    cross = jnp.dot(split_rows([v[:ROWS] for v in firsts]), along[...], preferred_element_type=F32)
+    for level in range(BATCH):
+        ratio_now = ratio[k + level]
+        response[k + level] = jnp.where(
+            k + level == 0, response[k + level], ratio_now * response[jnp.maximum(k + level - 1, 0)]
+        )
+        for f in range(FIELDS):
+            i = level * FIELDS + f
+            v = firsts[i]
+            straight = cross[16 * i:16 * i + 16] + cross[16 * (count + i):16 * (count + i) + 16]
+            total = (pltpu.roll(v, 23, 0) + pltpu.roll(v, 1, 0))[:ROWS] + (
+                straight + sides(side_first, start + i, ROWS)
+            )
+            mixed = value[start + i] + ratio_now * previous[f]
+            previous[f] = mixed
+            value[start + i] = mixed - VISCOSITY * (wet[:ROWS] * total)
 
 
 def exchange_kernel(
     out_hbm, state_hbm, mask_ref, depth_ref, scale_ref,
     base_hbm, response, forced, answered,
-    state, value, ratio, rims, mask_rims, packed, rim, wet_wide, previous, arrived, reply,
-    load_sem, store_sem, send_sem, recv_sem, own_sem, row_send, row_recv, edge_send, edge_recv,
+    state, value, ratio, rims, mask_rims, packed, rim, side_mask, side_state, side_first, wet_tall, along, previous,
+    arrived, reply, load_sem, store_sem, send_sem, recv_sem, own_sem, row_send, row_recv, edge_send, edge_recv,
 ):
     ox, oy = lax.axis_index("ox"), lax.axis_index("oy")
     me = ox * 8 + oy
@@ -252,26 +304,40 @@
     lax.fori_loop(1, DEVICES, greet, 0)
     pl.semaphore_wait(barrier, DEVICES - 1)
 
+    def rows_of(device, count):
+        return pl.ds(pl.multiple_of(device * PITCH, PITCH), count)
+
     def to_all(source, target, count, i):
+        mine = rows_of(me, count)
+
         def send(k, carry):
-            t, device = partner(k)
-            pltpu.make_async_remote_copy(
-                source.at[pl.ds(pl.multiple_of(t * PITCH, PITCH), count)],
-                target.at[pl.ds(pl.multiple_of(me * PITCH, PITCH), count)],
-                send_sem.at[i], recv_sem.at[i], device_id=device, device_id_type=MESH,
-            ).start()
+            dx, dy, dz = lax.rem(k, 4), lax.rem(k + k // 4, 4), lax.rem(k + k // 16, 4)
+            to_x = lax.rem(ox // 4 + dy, 4) * 4 + lax.rem(lax.rem(ox, 4) + dx, 4)
+            to_z = lax.rem(oy // 2 + dz, 4) * 2
+
+            def one(to_y):
+                pltpu.make_async_remote_copy(
+                    source.at[rows_of(to_x * 8 + to_y, count)], target.at[mine], send_sem.at[i], recv_sem.at[i],
+                    device_id=(to_x, to_y), device_id_type=MESH,
+                ).start()
+
+            one(to_z + lax.rem(oy + 1, 2))
+
+            @pl.when(k > 0)
+            def _():
+                one(to_z + lax.rem(oy, 2))
+
             return carry
 
-        lax.fori_loop(1, DEVICES, send, 0)
-        mine = pl.ds(pl.multiple_of(me * PITCH, PITCH), count)
+        lax.fori_loop(0, DEVICES // 2, send, 0)
         own = pltpu.make_async_copy(source.at[mine], target.at[mine], own_sem.at[i])
         own.start()
         return own
 
     def finish(source, target, count, i, own):
         rows = pl.ds(0, (DEVICES - 1) * count)
+        pltpu.make_async_copy(source.at[rows], target.at[rows], recv_sem.at[i]).wait()
         pltpu.make_async_copy(source.at[rows], target.at[rows], send_sem.at[i]).wait()
-        pltpu.make_async_copy(source.at[rows], target.at[rows], recv_sem.at[i]).wait()
         own.wait()
 
     own = to_all(out_hbm, arrived, SENT, 0)
@@ -304,10 +370,10 @@
     for load in loads:
         load.wait()
     pack_columns(state, mask_ref, packed)
-    for side, y in ((0, back), (1, ahead)):
-        edge(packed.at[side], rim.at[side, :, pl.ds(0, ROWS)], (ox, y))
-        edge(packed.at[side, :, pl.ds(0, 1)], rim.at[side, :, pl.ds(16, 1)], (up, y))
-        edge(packed.at[side, :, pl.ds(15, 1)], rim.at[side, :, pl.ds(23, 1)], (down, y))
+    for side, near in ((0, back), (1, ahead)):
+        edge(packed.at[side], rim.at[side, :, pl.ds(0, ROWS)], (ox, near))
+        edge(packed.at[side, :, pl.ds(0, 1)], rim.at[side, :, pl.ds(16, 1)], (up, near))
+        edge(packed.at[side, :, pl.ds(15, 1)], rim.at[side, :, pl.ds(23, 1)], (down, near))
 
     sweep_up(state, mask_ref, depth_ref, scale_ref, value, ratio, response.at[0])
 
@@ -317,20 +383,36 @@
     row8 = iota((8, COLS), 0)
     below = mask_rims[1].astype(F32) * (ox < 15).astype(F32)
     above = mask_rims[0].astype(F32) * (ox > 0).astype(F32)
-    tall = jnp.concatenate([wet, jnp.where(row8 < 4, below, above)], axis=0)
-    side = side_columns(rim, SLABS)
-    lane = iota((24, 128), 1)
+    wet_tall[...] = jnp.concatenate([wet, jnp.where(row8 < 4, below, above)], axis=0)
     row = iota((24, 128), 0)
-    ok = jnp.where(lane < 64, (oy < 7).astype(F32), (oy > 0).astype(F32))
-    ok = ok * jnp.where(row < 16, 1.0, jnp.where(row < 20, (ox < 15).astype(F32), (ox > 0).astype(F32)))
-    wet_wide[...] = jnp.concatenate([tall, side * ok], axis=1)
-    for copy in row_copies[:2]:
-        copy.wait()
+    inside = jnp.where(row < 16, 1.0, jnp.where(row < 20, (ox < 15).astype(F32), (ox > 0).astype(F32)))
+    side_mask[0] = inside * (oy < 7).astype(F32)
+    side_mask[1] = inside * (oy > 0).astype(F32)
+    side_setup(packed, rim, side_mask, side_state, side_first)
+    apart = iota((COLS, COLS), 0) - iota((COLS, COLS), 1)
+    along[...] = jnp.where(apart == 0, -4.0, jnp.where((apart == 1) | (apart == -1), 1.0, 0.0)).astype(BF16)
     level = functools.partial(
-        ocean_level, state=state, rims=rims, rim=rim, wet_wide=wet_wide, value=value, ratio=ratio,
-        response=response, previous=previous,
+        ocean_levels, state=state, rims=rims, side_state=side_state, side_first=side_first, wet_tall=wet_tall,
+        along=along, value=value, ratio=ratio, response=response, previous=previous,
     )
-    level(jnp.int32(0))
+
+    stores = []
+
+    def chunk_levels(c):
+        for copy in row_copies[2 * c:2 * c + 2]:
+            copy.wait()
+
+        def step(i, carry):
+            level(c * CHUNK_LEVELS + i * BATCH)
+            return carry
+
+        lax.fori_loop(0, CHUNK_LEVELS // BATCH, step, 0)
+        at = pl.ds(c * CHUNK, CHUNK)
+        stores.append(pltpu.make_async_copy(value.at[at], base_hbm.at[at], store_sem.at[c]))
+        stores[-1].start()
+
+    for c in range(EARLY):
+        chunk_levels(c)
 
     finish(out_hbm, arrived, SENT, 0, own)
     ids = arrived[pl.ds(STRIPS, 128, stride=PITCH), :]
@@ -361,21 +443,8 @@
             for j in range(2):
                 reply[pl.ds(j * 12 + strip, 128, stride=PITCH), :] = back_rows[j * 128:(j + 1) * 128]
     own = to_all(reply, answered, STRIPS, 1)
-
-    stores = []
-    for c in range(CHUNKS):
-        if c > 0:
-            for copy in row_copies[2 * c:2 * c + 2]:
-                copy.wait()
-
-        def step(k, carry):
-            level(k)
-            return carry
-
-        lax.fori_loop(max(1, c * CHUNK_LEVELS), (c + 1) * CHUNK_LEVELS, step, 0)
-        at = pl.ds(c * CHUNK, CHUNK)
-        stores.append(pltpu.make_async_copy(value.at[at], base_hbm.at[at], store_sem.at[c]))
-        stores[-1].start()
+    for c in range(EARLY, CHUNKS):
+        chunk_levels(c)
     finish(reply, answered, STRIPS, 1, own)
     for store in stores:
         store.wait()
@@ -403,7 +472,11 @@
             pltpu.VMEM((2, 8, COLS), jnp.int32),
             pltpu.VMEM((2, GROUPS, ROWS, 128), F32),
             pltpu.VMEM((2, GROUPS, 24, 128), F32),
-            pltpu.VMEM((24, 384), F32),
+            pltpu.VMEM((2, 24, 128), F32),
+            pltpu.VMEM((GROUPS, 24, 128), F32),
+            pltpu.VMEM((GROUPS, ROWS, 128), F32),
+            pltpu.VMEM((24, COLS), F32),
+            pltpu.VMEM((COLS, COLS), BF16),
             pltpu.VMEM((FIELDS, ROWS, COLS), F32),
             pltpu.VMEM((DEVICES * PITCH, 128), F32),
             pltpu.VMEM((DEVICES * PITCH, 128), F32),
@@ -411,7 +484,7 @@
             dma((CHUNKS, 2)), dma((CHUNKS, 2)), dma((8,)), dma((8,)),
         ],
         compiler_params=pltpu.CompilerParams(
-            collective_id=0, has_side_effects=True, vmem_limit_bytes=50 << 20
+            collective_id=0, has_side_effects=True, vmem_limit_bytes=LIMIT_R << 20
         ),
         name="exchange",
     )(outgoing, state, mask, depth, scale)
@@ -422,15 +495,18 @@
 LAST_LEVELS = LEVELS // LAST_STEPS
 
 
-def last_kernel(src_ref, weight_ref, base_ref, response_ref, forced_ref, answered_ref, dest_ref,
-                ocean_ref, surface_ref, rows, total):
+def last_kernel(src_ref, weight_hbm, base_hbm, response_ref, forced_ref, answered_ref, dest_ref,
+                ocean_ref, surface_ref, rows, total, weights, base_ref, sem, base_sem):
     step = pl.program_id(0)
 
     @pl.when(step == 0)
     def _():
+        for i in range(LAST_STEPS):
+            part_copy(base_hbm, base_ref, base_sem, i, LAST_LEVELS * FIELDS).start()
+            part_copy(weight_hbm, weights, sem, i, LAST_PAIRS).start()
         total[...] = jnp.zeros_like(total)
         rows[...] = jnp.zeros_like(rows)
-        down, across = column_square(dest_ref)
+        down, across = row_square(dest_ref)
         same = (down == across) & (iota((128, 128), 1) < iota((128, 128), 0))
         rank = jnp.sum(same.astype(F32), axis=1, keepdims=True)
         dest_here = down == iota((128, 128), 1).astype(F32)
@@ -447,19 +523,20 @@
                     jnp.dot(pick, hi, preferred_element_type=F32) + jnp.dot(pick, lo, preferred_element_type=F32)
                 )
 
+    part_copy(base_hbm, base_ref, base_sem, step, LAST_LEVELS * FIELDS).wait()
     for k in range(LAST_LEVELS):
         for f in range(FIELDS):
-            ocean_ref[k * FIELDS + f] = base_ref[k * FIELDS + f] + response_ref[k] * forced_ref[f]
+            slab = step * (LAST_LEVELS * FIELDS) + k * FIELDS + f
+            ocean_ref[k * FIELDS + f] = base_ref[slab] + response_ref[step * LAST_LEVELS + k] * forced_ref[f]
+    part_copy(weight_hbm, weights, sem, step, LAST_PAIRS).wait()
 
     for i in range(LAST_PAIRS):
         g = step * LAST_PAIRS + i
         row = jnp.concatenate(
             [rows[pl.ds(pl.multiple_of(h * 1024 + g * 8, 8), 8), :] for h in range(2)], axis=1
         )
-        hi = row.astype(BF16).astype(F32)
-        left = jnp.concatenate([hi, row - hi], axis=0).astype(BF16)
-        top, low = split2(weight_ref[i])
-        right = jnp.concatenate([top, low], axis=0)
+        left = split_rows([row])
+        right = jnp.concatenate(list(split2(weights[g])), axis=0)
         both = lax.dot_general(left, right, (((1,), (1,)), ((), ())), preferred_element_type=F32)
         both = both[:8] + both[8:]
         at = src_ref[g]
@@ -467,41 +544,47 @@
 
     @pl.when(step == LAST_STEPS - 1)
     def _():
-        surface_ref[...] = total[:, :FIELDS, :]
+        for f in range(FIELDS):
+            surface_ref[f] = total[:, f, :]
 
 
 def last_call(pair_weight, base, response, forced, answered, pair_src, pair_dest):
     whole = lambda shape: pl.BlockSpec(shape, lambda i, s: (0,) * len(shape))
     part = LAST_LEVELS * FIELDS
+    vmem = pl.BlockSpec(memory_space=pltpu.VMEM)
     return pl.pallas_call(
         last_kernel,
         out_shape=(
             jax.ShapeDtypeStruct((SLABS, ROWS, COLS), F32),
-            jax.ShapeDtypeStruct((BLOCKS, FIELDS, 128), F32),
+            jax.ShapeDtypeStruct((FIELDS, BLOCKS, 128), F32),
         ),
         grid_spec=pltpu.PrefetchScalarGridSpec(
             num_scalar_prefetch=1,
             grid=(LAST_STEPS,),
             in_specs=[
-                pl.BlockSpec((LAST_PAIRS, 128, COLS), lambda i, s: (i, 0, 0)),
-                pl.BlockSpec((part, ROWS, COLS), lambda i, s: (i, 0, 0)),
-                pl.BlockSpec((LAST_LEVELS, ROWS, COLS), lambda i, s: (i, 0, 0)),
-                whole((FIELDS, ROWS, COLS)),
-                whole((DEVICES * PITCH, 128)),
-                whole((PAIRS, 1)),
+                pl.BlockSpec(memory_space=pl.ANY),
+                pl.BlockSpec(memory_space=pl.ANY),
+                vmem,
+                vmem,
+                vmem,
+                vmem,
             ],
             out_specs=(
                 pl.BlockSpec((part, ROWS, COLS), lambda i, s: (i, 0, 0)),
-                whole((BLOCKS, FIELDS, 128)),
+                whole((FIELDS, BLOCKS, 128)),
             ),
             scratch_shapes=[
                 pltpu.VMEM((2048, 128), F32),
                 pltpu.VMEM((BLOCKS, 8, 128), F32),
+                pltpu.VMEM((PAIRS, 128, COLS), F32),
+                pltpu.VMEM((SLABS, ROWS, COLS), F32),
+                pltpu.SemaphoreType.DMA((LAST_STEPS,)),
+                pltpu.SemaphoreType.DMA((LAST_STEPS,)),
             ],
         ),
-        compiler_params=pltpu.CompilerParams(vmem_limit_bytes=40 << 20),
+        compiler_params=pltpu.CompilerParams(vmem_limit_bytes=LIMIT_L << 20),
         name="outputs",
-    )(pair_src, pair_weight, base, response, forced, answered, pair_dest)
+    )(pair_src, pair_weight, base, response, forced, answered, pair_dest.reshape(1, PAIRS))
 
 
 def shards(atm_flux, pair_weight, pair_src, pair_dest, pair_block, ocean_state, land_mask, kpp_depth, mixing_scale):
@@ -509,7 +592,7 @@
     state = ocean_state.reshape(SLABS, ROWS, COLS)
     base, response, forced, answered = exchange_call(outgoing, state, land_mask, kpp_depth, mixing_scale)
     ocean, surface = last_call(pair_weight, base, response, forced, answered, pair_src, pair_dest)
-    return ocean.reshape(LEVELS, FIELDS, ROWS, COLS), surface
+    return ocean.reshape(LEVELS, FIELDS, ROWS, COLS), jnp.transpose(surface, (1, 0, 2))
 
 
 def solution(mesh):

time: 135 us -> 111 us (0.82)
  local copies, waits for them, and re-layouts: 12.8 us -> 0 us
  Pallas kernels: 121 us -> 110 us
    unnamed x21 -> x0, local copies, waits for them, and re-layouts: 12.8 us -> none
    pallas_call x1, Pallas kernels: 97.8 us -> 86.6 us  [exchange_call(): pl.pallas_call(exchange_kernel, out_shape=(jax.ShapeDtypeStruct((SLABS, R...]
    pallas_call x1, Pallas kernels: 5.65 us -> 9.47 us  [flux_call(): pl.pallas_call(flux_kernel, out_shape=jax.ShapeDtypeStruct((DEVICES * PIT...]
    pallas_call x1, Pallas kernels: 17.1 us -> 14.1 us  [last_call(): pl.pallas_call(last_kernel, out_shape=(jax.ShapeDtypeStruct((SLABS, ROWS,...]
where the time goes in v2:
time: 111 us
  Pallas kernels  110 us (99%)
    pallas_call x1, Pallas kernels, exchange_call(): pl.pallas_call(exchange_kernel, out_shape=(jax.ShapeDtypeStruct((SLABS, R...  86.6 us
    pallas_call x1, Pallas kernels, last_call(): pl.pallas_call(last_kernel, out_shape=(jax.ShapeDtypeStruct((SLABS, ROWS,...  14.1 us
    pallas_call x1, Pallas kernels, flux_call(): pl.pallas_call(flux_kernel, out_shape=jax.ShapeDtypeStruct((DEVICES * PIT...  9.47 us

profile of v2, /device:TPU:1, one launch (start us, length us, event | category | flops | bytes accessed | tf_op | source)
XLA Modules:
  0.0 110.8 jit_solution(10374171918150785331)
XLA Ops:
  0.6 9.5 %contributions.1.out_hbm = f32[4096,128]{1,0:T(8,128)} custom-call(s32[96]{0:T(128)} %src_ref.3, f32[96,128,256]{2,1,0:T(8,128)} %weight_hbm.3, f32[6,32,128]{2,1,0:T(8,128)} %bitcast.7, s32[1,96]{1,0:T(1,128)} %bitcast.8, s32[1,96]{1,0:T(1,128)} %bitcast.10), custom_call_target="tpu_custom_call" | custom-call | tf_op jit(solution)/shard_map/contributions/pallas_call | solution.py:116
  10.1 86.6 %exchange.1 = (f32[480,16,256]{2,1,0:T(8,128)}, f32[80,16,256]{2,1,0:T(8,128)}, f32[6,16,256]{2,1,0:T(8,128)}, f32[4096,128]{1,0:T(8,128)}) custom-call(f32[4096,128]{1,0:T(8,128)} %contributions.1.out_hbm, f32[480,16,256]{2,1,0:T(8,128)} %bitcast.6, s32[16,256]{1,0:T(8,128)} %mask_ref.1, s32[16,256]{1,0:T(8,128)} %depth_ref.1, f32[16,256]{1,0:T(8,128)} %scale_ref.1), custom_call_target="tpu_custom_call" | custom-call | tf_op jit(solution)/shard_map/exchange/pallas_call | solution.py:457
  96.7 14.1 %outputs.1 = (f32[480,16,256]{2,1,0:T(8,128)}, f32[6,32,128]{2,1,0:T(8,128)}) custom-call(s32[96]{0:T(128)} %src_ref.3, f32[96,128,256]{2,1,0:T(8,128)} %weight_hbm.3, f32[480,16,256]{2,1,0:T(8,128)} %get-tuple-element.8.base_hbm, f32[80,16,256]{2,1,0:T(8,128)} %get-tuple-element.9.response_ref, f32[6,16,256]{2,1,0:T(8,128)} %get-tuple-element.10.forced_ref, ...), custom_call_target="tpu_custom_call" | custom-call | tf_op jit(solution)/shard_map/outputs/pallas_call | solution.py:555

commit v3 on v2

--- a/solution.py
+++ b/solution.py
@@ -28,11 +28,11 @@
 GROUP = 64
 GROUPS = 8
 CHUNKS = 5
-EARLY = 2
+BOUNDS = (0, 4, 24, 44, 64, 80)
+EARLY = 1
 BATCH = 4
-LIMIT_R = 54
+LIMIT_R = 58
 LIMIT_L = 58
-CHUNK_LEVELS = LEVELS // CHUNKS
 CHUNK = SLABS // CHUNKS
 
 
@@ -60,82 +60,51 @@
     return pltpu.make_async_copy(weight_hbm.at[at], weights.at[at], sem.at[i])
 
 
-def flux_kernel(src_ref, weight_hbm, flux_ref, dest_ref, block_ref, out_ref, parts, contrib, weights, sem):
-    step = pl.program_id(0)
-
-    @pl.when(step == 0)
-    def _():
-        for i in range(PAIRS // FLUX_STEP):
-            part_copy(weight_hbm, weights, sem, i, FLUX_STEP).start()
-        contrib[...] = jnp.zeros_like(contrib)
-
-        def prepare(b, carry):
-            rows = jnp.concatenate([flux_ref[:, b, :], jnp.zeros((2, 128), F32)], axis=0)
-            hi = rows.astype(BF16).astype(F32)
-            both = jnp.concatenate([hi, rows - hi], axis=0).astype(BF16)
-            parts[b] = jnp.concatenate([both, both], axis=1)
-            return carry
-
-        lax.fori_loop(0, BLOCKS, prepare, 0)
-
-    part_copy(weight_hbm, weights, sem, step, FLUX_STEP).wait()
-    for i in range(FLUX_STEP):
-        g = step * FLUX_STEP + i
-        left = parts[src_ref[g]]
-        hi, lo = split2(weights[g])
-        right = jnp.concatenate([hi, lo], axis=0)
-        both = jnp.dot(left, right, preferred_element_type=F32)
-        value = both[:8] + both[8:]
-        at = pl.multiple_of(g * 8, 8)
-        contrib[pl.ds(at, 8), :] = value[:, :128]
-        contrib[pl.ds(pl.multiple_of(1024 + g * 8, 8), 8), :] = value[:, 128:]
-
-    @pl.when(step == pl.num_programs(0) - 1)
-    def _():
-        down, across = row_square(dest_ref)
-        same = (down == across) & (iota((128, 128), 0) < iota((128, 128), 1))
-        rank = jnp.sum(same.astype(F32), axis=0, keepdims=True)
-        dest_here = across == iota((128, 128), 0).astype(F32)
-        places = [dest_here & (rank == float(j)) for j in range(2)]
-        rows = jnp.concatenate([block_ref[...].astype(F32), jnp.zeros((1, 128 - PAIRS), F32)], axis=1) + 1.0
-        ids = [jnp.sum(jnp.where(p, rows, 0.0), axis=1, keepdims=True) - 1.0 for p in places]
-        lane = iota((128, 128), 1)
-        out_ref[pl.ds(STRIPS, 128, stride=PITCH), :] = jnp.where(lane == 0, ids[0], ids[1])
-        place = jnp.concatenate([p.astype(F32).astype(BF16) for p in places], axis=0)
-        place = jnp.concatenate([place, place], axis=1)
-        for f in range(FIELDS):
-            for h in range(2):
-                hi, lo = split2(contrib[pl.ds(h * 1024 + f, 128, stride=8), :])
-                got = jnp.dot(place, jnp.concatenate([hi, lo], axis=0), preferred_element_type=F32)
-                for j in range(2):
-                    out_ref[pl.ds(j * 12 + 2 * f + h, 128, stride=PITCH), :] = got[j * 128:(j + 1) * 128]
-
-
-def flux_call(pair_weight, atm_flux, pair_src, pair_dest, pair_block):
-    whole = lambda shape: pl.BlockSpec(shape, lambda i, s: (0,) * len(shape))
-    return pl.pallas_call(
-        flux_kernel,
-        out_shape=jax.ShapeDtypeStruct((DEVICES * PITCH, 128), F32),
-        grid_spec=pltpu.PrefetchScalarGridSpec(
-            num_scalar_prefetch=1,
-            grid=(PAIRS // FLUX_STEP,),
-            in_specs=[
-                pl.BlockSpec(memory_space=pl.ANY),
-                whole((FIELDS, BLOCKS, 128)),
-                whole((1, PAIRS)),
-                whole((1, PAIRS)),
-            ],
-            out_specs=whole((DEVICES * PITCH, 128)),
-            scratch_shapes=[
-                pltpu.VMEM((BLOCKS, 16, 256), BF16),
-                pltpu.VMEM((2048, 128), F32),
-                pltpu.VMEM((PAIRS, 128, COLS), F32),
-                pltpu.SemaphoreType.DMA((PAIRS // FLUX_STEP,)),
-            ],
-        ),
-        compiler_params=pltpu.CompilerParams(vmem_limit_bytes=56 << 20),
-        name="contributions",
-    )(pair_src, pair_weight, jnp.transpose(atm_flux, (1, 0, 2)), pair_dest.reshape(1, PAIRS), pair_block.reshape(1, PAIRS))
+def contributions(src_ref, weight_hbm, flux_ref, dest_ref, block_ref, out_ref, parts, contrib, weights, sem):
+    contrib[...] = jnp.zeros_like(contrib)
+
+    def prepare(b, carry):
+        rows = jnp.concatenate([flux_ref[:, b, :], jnp.zeros((2, 128), F32)], axis=0)
+        hi = rows.astype(BF16).astype(F32)
+        both = jnp.concatenate([hi, rows - hi], axis=0).astype(BF16)
+        parts[b] = jnp.concatenate([both, both], axis=1)
+        return carry
+
+    lax.fori_loop(0, BLOCKS, prepare, 0)
+
+    def some(step, carry):
+        part_copy(weight_hbm, weights, sem, step, FLUX_STEP).wait()
+        for i in range(FLUX_STEP):
+            g = step * FLUX_STEP + i
+            left = parts[src_ref[g]]
+            hi, lo = split2(weights[g])
+            right = jnp.concatenate([hi, lo], axis=0)
+            both = jnp.dot(left, right, preferred_element_type=F32)
+            value = both[:8] + both[8:]
+            at = pl.multiple_of(g * 8, 8)
+            contrib[pl.ds(at, 8), :] = value[:, :128]
+            contrib[pl.ds(pl.multiple_of(1024 + g * 8, 8), 8), :] = value[:, 128:]
+        return carry
+
+    lax.fori_loop(0, PAIRS // FLUX_STEP, some, 0)
+
+    down, across = row_square(dest_ref)
+    same = (down == across) & (iota((128, 128), 0) < iota((128, 128), 1))
+    rank = jnp.sum(same.astype(F32), axis=0, keepdims=True)
+    dest_here = across == iota((128, 128), 0).astype(F32)
+    places = [dest_here & (rank == float(j)) for j in range(2)]
+    rows = jnp.concatenate([block_ref[...].astype(F32), jnp.zeros((1, 128 - PAIRS), F32)], axis=1) + 1.0
+    ids = [jnp.sum(jnp.where(p, rows, 0.0), axis=1, keepdims=True) - 1.0 for p in places]
+    lane = iota((128, 128), 1)
+    out_ref[pl.ds(STRIPS, 128, stride=PITCH), :] = jnp.where(lane == 0, ids[0], ids[1])
+    place = jnp.concatenate([p.astype(F32).astype(BF16) for p in places], axis=0)
+    place = jnp.concatenate([place, place], axis=1)
+    for f in range(FIELDS):
+        for h in range(2):
+            hi, lo = split2(contrib[pl.ds(h * 1024 + f, 128, stride=8), :])
+            got = jnp.dot(place, jnp.concatenate([hi, lo], axis=0), preferred_element_type=F32)
+            for j in range(2):
+                out_ref[pl.ds(j * 12 + 2 * f + h, 128, stride=PITCH), :] = got[j * 128:(j + 1) * 128]
 
 
 def pack_columns(state, mask_ref, packed):
@@ -275,9 +244,14 @@
             value[start + i] = mixed - VISCOSITY * (wet[:ROWS] * total)
 
 
+def span(c):
+    return pl.ds(BOUNDS[c] * FIELDS, (BOUNDS[c + 1] - BOUNDS[c]) * FIELDS)
+
+
 def exchange_kernel(
-    out_hbm, state_hbm, mask_ref, depth_ref, scale_ref,
+    src_ref, weight_hbm, flux_ref, dest_ref, block_ref, state_hbm, mask_ref, depth_ref, scale_ref,
     base_hbm, response, forced, answered,
+    out_ref, parts, contrib, weights, weight_sem,
     state, value, ratio, rims, mask_rims, packed, rim, side_mask, side_state, side_first, wet_tall, along, previous,
     arrived, reply, load_sem, store_sem, send_sem, recv_sem, own_sem, row_send, row_recv, edge_send, edge_recv,
 ):
@@ -289,6 +263,8 @@
         loads.append(pltpu.make_async_copy(state_hbm.at[at], state.at[at], load_sem.at[c]))
         loads[-1].start()
 
+    for i in range(PAIRS // FLUX_STEP):
+        part_copy(weight_hbm, weights, weight_sem, i, FLUX_STEP).start()
     barrier = pltpu.get_barrier_semaphore()
 
     def partner(k):
@@ -340,13 +316,12 @@
         pltpu.make_async_copy(source.at[rows], target.at[rows], send_sem.at[i]).wait()
         own.wait()
 
-    own = to_all(out_hbm, arrived, SENT, 0)
 
     up, down = lax.rem(ox + 15, 16), lax.rem(ox + 1, 16)
     back, ahead = lax.rem(oy + 7, 8), lax.rem(oy + 1, 8)
     row_copies = []
     for c in range(CHUNKS):
-        at = pl.ds(c * CHUNK, CHUNK)
+        at = span(c)
         for d, (mine, there, device) in enumerate(((14, 6, down), (0, 0, up))):
             copy = pltpu.make_async_remote_copy(
                 state_hbm.at[at, pl.ds(mine, 2)], rims.at[at, pl.ds(there, 2)],
@@ -375,6 +350,8 @@
         edge(packed.at[side, :, pl.ds(0, 1)], rim.at[side, :, pl.ds(16, 1)], (up, near))
         edge(packed.at[side, :, pl.ds(15, 1)], rim.at[side, :, pl.ds(23, 1)], (down, near))
 
+    contributions(src_ref, weight_hbm, flux_ref, dest_ref, block_ref, out_ref, parts, contrib, weights, weight_sem)
+    own = to_all(out_ref, arrived, SENT, 0)
     sweep_up(state, mask_ref, depth_ref, scale_ref, value, ratio, response.at[0])
 
     for copy in edge_copies:
@@ -403,18 +380,18 @@
             copy.wait()
 
         def step(i, carry):
-            level(c * CHUNK_LEVELS + i * BATCH)
+            level(BOUNDS[c] + i * BATCH)
             return carry
 
-        lax.fori_loop(0, CHUNK_LEVELS // BATCH, step, 0)
-        at = pl.ds(c * CHUNK, CHUNK)
+        lax.fori_loop(0, (BOUNDS[c + 1] - BOUNDS[c]) // BATCH, step, 0)
+        at = span(c)
         stores.append(pltpu.make_async_copy(value.at[at], base_hbm.at[at], store_sem.at[c]))
         stores[-1].start()
 
     for c in range(EARLY):
         chunk_levels(c)
 
-    finish(out_hbm, arrived, SENT, 0, own)
+    finish(out_ref, arrived, SENT, 0, own)
     ids = arrived[pl.ds(STRIPS, 128, stride=PITCH), :]
     ids = jnp.concatenate([ids[:, 0:1], ids[:, 1:2]], axis=0)
     lane = iota((256, 128), 1)
@@ -450,7 +427,7 @@
         store.wait()
 
 
-def exchange_call(outgoing, state, mask, depth, scale):
+def exchange_call(pair_src, pair_weight, atm_flux, pair_dest, pair_block, state, mask, depth, scale):
     vmem = pl.BlockSpec(memory_space=pltpu.VMEM)
     anywhere = pl.BlockSpec(memory_space=pl.ANY)
     dma = pltpu.SemaphoreType.DMA
@@ -462,9 +439,14 @@
             jax.ShapeDtypeStruct((FIELDS, ROWS, COLS), F32),
             jax.ShapeDtypeStruct((DEVICES * PITCH, 128), F32),
         ),
-        in_specs=[anywhere, anywhere, vmem, vmem, vmem],
+        in_specs=[pl.BlockSpec(memory_space=pltpu.SMEM), anywhere, vmem, vmem, vmem, anywhere, vmem, vmem, vmem],
         out_specs=(anywhere, vmem, vmem, vmem),
         scratch_shapes=[
+            pltpu.VMEM((DEVICES * PITCH, 128), F32),
+            pltpu.VMEM((BLOCKS, 16, 256), BF16),
+            pltpu.VMEM((2048, 128), F32),
+            pltpu.VMEM((PAIRS, 128, COLS), F32),
+            dma((PAIRS // FLUX_STEP,)),
             pltpu.VMEM((SLABS, ROWS, COLS), F32),
             pltpu.VMEM((SLABS, ROWS, COLS), F32),
             pltpu.VMEM((LEVELS, ROWS, COLS), F32),
@@ -487,7 +469,10 @@
             collective_id=0, has_side_effects=True, vmem_limit_bytes=LIMIT_R << 20
         ),
         name="exchange",
-    )(outgoing, state, mask, depth, scale)
+    )(
+        pair_src, pair_weight, jnp.transpose(atm_flux, (1, 0, 2)), pair_dest.reshape(1, PAIRS),
+        pair_block.reshape(1, PAIRS), state, mask, depth, scale,
+    )
 
 
 LAST_STEPS = 16
@@ -588,9 +573,10 @@
 
 
 def shards(atm_flux, pair_weight, pair_src, pair_dest, pair_block, ocean_state, land_mask, kpp_depth, mixing_scale):
-    outgoing = flux_call(pair_weight, atm_flux, pair_src, pair_dest, pair_block)
     state = ocean_state.reshape(SLABS, ROWS, COLS)
-    base, response, forced, answered = exchange_call(outgoing, state, land_mask, kpp_depth, mixing_scale)
+    base, response, forced, answered = exchange_call(
+        pair_src, pair_weight, atm_flux, pair_dest, pair_block, state, land_mask, kpp_depth, mixing_scale
+    )
     ocean, surface = last_call(pair_weight, base, response, forced, answered, pair_src, pair_dest)
     return ocean.reshape(LEVELS, FIELDS, ROWS, COLS), jnp.transpose(surface, (1, 0, 2))
 

time: 111 us -> 98.2 us (0.88)
  Pallas kernels: 110 us -> 97.4 us
    pallas_call x1 -> x0, Pallas kernels: 9.47 us -> none  [flux_call(): pl.pallas_call(flux_kernel, out_shape=jax.ShapeDtypeStruct((DEVICES * PIT...]
    pallas_call x1, Pallas kernels: 86.6 us -> 83.3 us  [exchange_call(): pl.pallas_call(exchange_kernel, out_shape=(jax.ShapeDtypeStruct((SLABS, R...]
where the time goes in v3:
time: 98.2 us; the launch traced here: 98 us
  Pallas kernels  97.4 us (99%)
    pallas_call x1, Pallas kernels, exchange_call(): pl.pallas_call(exchange_kernel, out_shape=(jax.ShapeDtypeStruct((SLABS, R...  83.3 us
    pallas_call x1, Pallas kernels, last_call(): pl.pallas_call(last_kernel, out_shape=(jax.ShapeDtypeStruct((SLABS, ROWS,...  14.1 us

profile of v3, /device:TPU:1, one launch (start us, length us, event | category | flops | bytes accessed | tf_op | source)
XLA Modules:
  0.0 98.0 jit_solution(15396681320139789558)
XLA Ops:
  0.6 83.3 %exchange.1 = (f32[480,16,256]{2,1,0:T(8,128)}, f32[80,16,256]{2,1,0:T(8,128)}, f32[6,16,256]{2,1,0:T(8,128)}, f32[4096,128]{1,0:T(8,128)}) custom-call(s32[96]{0:T(128)} %src_ref.3, f32[96,128,256]{2,1,0:T(8,128)} %weight_hbm.3, f32[6,32,128]{2,1,0:T(8,128)} %bitcast.7, s32[1,96]{1,0:T(1,128)} %bitcast.8, s32[1,96]{1,0:T(1,128)} %bitcast.10, ...), custom_call_target="tpu_custom_call" | custom-call | tf_op jit(solution)/shard_map/exchange/pallas_call | solution.py:434
  83.9 14.1 %outputs.1 = (f32[480,16,256]{2,1,0:T(8,128)}, f32[6,32,128]{2,1,0:T(8,128)}) custom-call(s32[96]{0:T(128)} %src_ref.3, f32[96,128,256]{2,1,0:T(8,128)} %weight_hbm.3, f32[480,16,256]{2,1,0:T(8,128)} %get-tuple-element.8.base_hbm, f32[80,16,256]{2,1,0:T(8,128)} %get-tuple-element.9.response_ref, f32[6,16,256]{2,1,0:T(8,128)} %get-tuple-element.10.forced_ref, ...), custom_call_target="tpu_custom_call" | custom-call | tf_op jit(solution)/shard_map/outputs/pallas_call | solution.py:540
